TPU v7x, 32 devices: a whole 2x2x4 slice. The times are simulated.
32 devices in a mesh: pipe: 2 (over x), ctx: 8 (over z, y), tp: 2 (over core).
Axes of the slice: x: 2, y: 2, z: 4, core: 2. Of those that a mesh axis runs over, the one named last changes fastest.
Arguments:
- resid_in: bfloat16 [1024, 4096], P('ctx', 'tp'), may hold values from -6 to 6
- ssm_input: bfloat16 [1024, 8192], P('ctx', 'tp'), may hold values from -6 to 6
- ssm_gate: bfloat16 [1024, 8192], P('ctx', 'tp'), may hold values from -6 to 6
- ssm_in_b: bfloat16 [1024, 512], P('ctx', 'tp'), may hold values from -0.5 to 0.5
- ssm_out_c: bfloat16 [1024, 512], P('ctx', 'tp'), may hold values from -6 to 6
- step_size: float32 [1024, 128], P('ctx', 'tp'), as said below
- decay_rate: float32 [128], P('tp'), may hold values from 0.0001 to 1, as said below
- skip_gain: float32 [128], P('tp'), may hold values from 0.5 to 1.5
- norm_gain: float32 [8192], P('tp'), may hold values from 0.1 to 1.9
- queries: bfloat16 [1024, 8192], P('ctx', 'tp'), may hold values from -6 to 6
- keys: bfloat16 [1024, 512], P('ctx', 'tp'), may hold values from -6 to 6
- values: bfloat16 [1024, 512], P('ctx', 'tp'), may hold values from -6 to 6
- out_weights: bfloat16 [2, 8192, 4096], P('pipe', 'tp', 'ctx'), may hold values from -0.0625 to 0.0625
Outputs:
- sections_out: bfloat16 [2, 1024, 4096], P('pipe', 'ctx', 'tp')
Inputs may be any that keep to these rules, and one draw needn't show every extreme that they name: `step_size`: step sizes are positive. `decay_rate`: rates are positive.
All inputs are finite; a program needn't handle non-finite values.
Results may differ from a plain program's by a relative error of at most 0.015.
Values may be sent and summed in bfloat16 or wider, within the bound.
A program may use at most 256 MiB of HBM per device.

v0:
```python
import math

import jax
import jax.numpy as jnp
from jax import lax
from jax.sharding import PartitionSpec as P

MHEAD_DIM = 64
STATE = 128
SCAN_BLOCK = 128
HEAD_DIM = 128


exact_mode = lax.Precision.HIGHEST
norm_eps = 1e-05


def entering_2(x, axis, combine, identity):
    peers, position = (lax.axis_size(axis), lax.axis_index(axis))
    everything = jax.tree.map(
        lambda part, kind: lax.all_gather(part.astype(kind), axis), x, (jnp.bfloat16, jnp.bfloat16)
    )
    start = jax.tree.map(
        lambda part, zero: jnp.broadcast_to(jnp.asarray(zero, part.dtype), part.shape), x, identity
    )

    def turn(k, before):
        reached = k < position
        new = combine(
            before, jax.tree.map(lambda part, own: part[k].astype(own.dtype), everything, x)
        )
        return jax.tree.map(lambda a, b: jnp.where(reached, a, b), new, before)

    return lax.fori_loop(0, peers, turn, start)


def from_partner(block, axis, distance):
    count = lax.axis_size(axis)
    route = []
    for low in range(count):
        high = low | 1 << distance
        if high != low and high < count:
            route += [(low, high), (high, low)]
    return lax.ppermute(block, axis, route)


def shifted(x, axis, by):
    peers = lax.axis_size(axis)
    pairs = [(i, i + by) for i in range(peers) if 0 <= i + by < peers]
    return lax.ppermute(x, axis, pairs)


def block_scan(state_now, inputs_x, input_b, output_c, step_rows, log_decay):
    width = inputs_x.shape[0]
    groups = inputs_x.shape[1]
    per_group = inputs_x.shape[2]
    running = jnp.cumsum(log_decay, axis=0)
    spread = running[:, None, :] - running[None, :, :]
    causal = (
        jnp.arange(width, dtype=jnp.int32)[:, None] >= jnp.arange(width, dtype=jnp.int32)[None, :]
    )
    decay_mat = jnp.exp(jnp.where(causal[:, :, None], spread, -jnp.inf))
    decay_mat = decay_mat.reshape(width, width, groups, per_group).transpose(2, 3, 0, 1)
    cross_cb = jnp.einsum("tgn,sgn->gts", output_c, input_b, precision=exact_mode)
    step_cols = step_rows.reshape(width, groups, per_group).transpose(1, 2, 0)
    mixing = cross_cb[:, None, :, :] * decay_mat * step_cols[:, :, None, :]
    within = jnp.einsum("gjts,sgjp->tgjp", mixing, inputs_x, precision=exact_mode)
    entry = jnp.exp(running).reshape(width, groups, per_group)
    carried = (
        jnp.einsum("tgn,gjpn->tgjp", output_c, state_now, precision=exact_mode)
        * entry[:, :, :, None]
    )
    tail_weight = (jnp.exp(running[-1][None, :] - running) * step_rows).reshape(
        width, groups, per_group
    )
    leaving = jnp.exp(running[-1]).reshape(groups, per_group)
    state_next = leaving[:, :, None, None] * state_now + jnp.einsum(
        "sgj,sgjp,sgn->gjpn", tail_weight, inputs_x, input_b, precision=exact_mode
    )
    return (state_next, within + carried)


def gate_norm(values_y, gate_in, gains, groups):
    rows_here = values_y.shape[0]
    gated = values_y * jax.nn.silu(gate_in.astype(jnp.float32))
    grouped = gated.reshape(rows_here, groups, -1)
    meansq = jnp.mean(grouped * grouped, axis=-1, keepdims=True)
    scaled = (grouped * lax.rsqrt(meansq + norm_eps)).reshape(rows_here, -1)
    return (scaled * gains[None, :]).astype(jnp.bfloat16)


def join_states(earlier, later):
    return (earlier[0] * later[0], later[0][:, :, None, None] * earlier[1] + later[1])


def mamba_mixer(
    ssm_input, ssm_gate, ssm_in_b, ssm_out_c, step_size, decay_rate, skip_gain, norm_gain
):
    rows_here = ssm_input.shape[0]
    head_count = decay_rate.shape[0]
    groups = ssm_in_b.shape[1] // STATE
    per_group = head_count // groups
    block_count = rows_here // SCAN_BLOCK
    log_decay = -step_size * decay_rate[None, :]
    inputs_x = ssm_input.reshape(block_count, SCAN_BLOCK, groups, per_group, MHEAD_DIM)
    input_b = ssm_in_b.reshape(block_count, SCAN_BLOCK, groups, STATE)
    output_c = ssm_out_c.reshape(block_count, SCAN_BLOCK, groups, STATE)

    def block_turn(state_now, block_data):
        part_x, part_b, part_c, part_step, part_log = block_data
        return block_scan(
            state_now,
            part_x.astype(jnp.float32),
            part_b.astype(jnp.float32),
            part_c.astype(jnp.float32),
            part_step,
            part_log,
        )

    start_state = jnp.zeros((groups, per_group, MHEAD_DIM, STATE), jnp.float32)
    local_state, pieces = lax.scan(
        block_turn,
        start_state,
        (
            inputs_x,
            input_b,
            output_c,
            step_size.reshape(block_count, SCAN_BLOCK, head_count),
            log_decay.reshape(block_count, SCAN_BLOCK, head_count),
        ),
    )
    running = jnp.cumsum(log_decay, axis=0)
    through = jnp.exp(running[-1]).reshape(groups, per_group)
    prior = entering_2(
        (through, local_state),
        "ctx",
        join_states,
        (jnp.ones_like(through), jnp.zeros_like(local_state)),
    )
    entering = prior[1]
    output_all = ssm_out_c.astype(jnp.float32).reshape(rows_here, groups, STATE)
    carried = (
        jnp.einsum("tgn,gjpn->tgjp", output_all, entering, precision=exact_mode)
        * jnp.exp(running).reshape(rows_here, groups, per_group)[:, :, :, None]
    )
    skipped = (
        ssm_input.astype(jnp.float32).reshape(rows_here, groups, per_group, MHEAD_DIM)
        * skip_gain.reshape(groups, per_group)[None, :, :, None]
    )
    values_y = pieces.reshape(rows_here, groups, per_group, MHEAD_DIM) + carried + skipped
    return gate_norm(values_y.reshape(rows_here, -1), ssm_gate, norm_gain, groups)


def attention(queries, keys, values, ctx_rank):
    rows_here = queries.shape[0]
    kv_count = keys.shape[1] // HEAD_DIM
    per_key = queries.shape[1] // HEAD_DIM // kv_count
    query_groups = queries.reshape(rows_here, kv_count, per_key, HEAD_DIM)
    query_pos = ctx_rank * rows_here + jnp.arange(rows_here, dtype=jnp.int32)
    last_query = query_pos[-1]
    score_scale = 1.0 / math.sqrt(HEAD_DIM)

    def key_block(running, block_data):
        key_rows, value_rows, first_key = block_data

        def absorb(held):
            row_max, row_sum, weighted = held
            scores = (
                jnp.einsum(
                    "qgjd,kgd->gjqk", query_groups, key_rows, preferred_element_type=jnp.float32
                )
                * score_scale
            )
            key_pos = first_key + jnp.arange(key_rows.shape[0], dtype=jnp.int32)
            allowed = key_pos[None, :] <= query_pos[:, None]
            scores = jnp.where(allowed, scores, -1e30)
            new_max = jnp.maximum(row_max, jnp.max(scores, axis=-1))
            rescale = jnp.exp(row_max - new_max)
            weights_exp = jnp.where(allowed, jnp.exp(scores - new_max[..., None]), 0.0)
            row_sum = row_sum * rescale + jnp.sum(weights_exp, axis=-1)
            weighted = weighted * rescale[..., None] + jnp.einsum(
                "gjqk,kgd->gjqd",
                weights_exp.astype(jnp.bfloat16),
                value_rows,
                preferred_element_type=jnp.float32,
            )
            return (new_max, row_sum, weighted)

        return (lax.cond(first_key <= last_query, absorb, lambda held: held, running), None)

    start_state = (
        jnp.full((kv_count, per_key, rows_here), -1e30, jnp.float32),
        jnp.zeros((kv_count, per_key, rows_here), jnp.float32),
        jnp.zeros((kv_count, per_key, rows_here, HEAD_DIM), jnp.float32),
    )
    running = start_state
    key_piece = lax.all_gather(keys, "ctx", axis=0, tiled=True)
    value_piece = lax.all_gather(values, "ctx", axis=0, tiled=True)
    count = key_piece.shape[0]
    width = math.gcd(count, 1024)
    blocks = count // width
    key_rows = key_piece.reshape(blocks, width, kv_count, HEAD_DIM)
    value_rows = value_piece.reshape(blocks, width, kv_count, HEAD_DIM)
    starts = width * jnp.arange(blocks, dtype=jnp.int32)
    running, unused = lax.scan(key_block, running, (key_rows, value_rows, starts))
    row_max, row_sum, weighted = running
    mixed = (weighted / row_sum[..., None]).transpose(2, 0, 1, 3).reshape(rows_here, -1)
    return mixed.astype(jnp.bfloat16)


def take_half(array, axis_dim, section):
    width = array.shape[axis_dim] // 2
    return lax.dynamic_slice_in_dim(array, section * width, width, axis_dim)


def per_device(
    resid_in,
    ssm_input,
    ssm_gate,
    ssm_in_b,
    ssm_out_c,
    step_size,
    decay_rate,
    skip_gain,
    norm_gain,
    queries,
    keys,
    values,
    out_weights,
):
    section = lax.axis_index("pipe")
    ctx_rank = lax.axis_index("ctx")
    mamba_part = mamba_mixer(
        take_half(ssm_input, 1, section),
        take_half(ssm_gate, 1, section),
        take_half(ssm_in_b, 1, section),
        take_half(ssm_out_c, 1, section),
        take_half(step_size, 1, section),
        take_half(decay_rate, 0, section),
        take_half(skip_gain, 0, section),
        take_half(norm_gain, 0, section),
    )
    attn_part = attention(
        take_half(queries, 1, section),
        take_half(keys, 1, section),
        take_half(values, 1, section),
        ctx_rank,
    )
    outgoing = jnp.where(section == 0, attn_part, mamba_part)
    kept_half = jnp.where(section == 0, mamba_part, attn_part)
    incoming = from_partner(outgoing, "pipe", 0)
    mixed_rows = jnp.where(
        section == 0,
        jnp.concatenate([kept_half, incoming], axis=1),
        jnp.concatenate([incoming, kept_half], axis=1),
    )
    partial_value = jnp.dot(
        mixed_rows,
        lax.all_gather(out_weights, "ctx", axis=2, tiled=True)[0],
        preferred_element_type=jnp.float32,
    )
    projected = lax.psum_scatter(
        partial_value.astype(jnp.bfloat16), "tp", scatter_dimension=1, tiled=True
    ).astype(jnp.float32)
    own_section = (resid_in.astype(jnp.float32) + projected).astype(jnp.bfloat16)
    received = shifted(own_section, "pipe", 1)
    second_section = (received.astype(jnp.float32) + projected).astype(jnp.bfloat16)
    return jnp.where(section == 0, own_section, second_section)[None]


def solution(mesh):
    return jax.shard_map(
        per_device,
        mesh=mesh,
        in_specs=(
            P("ctx", "tp"),
            P("ctx", "tp"),
            P("ctx", "tp"),
            P("ctx", "tp"),
            P("ctx", "tp"),
            P("ctx", "tp"),
            P("tp"),
            P("tp"),
            P("tp"),
            P("ctx", "tp"),
            P("ctx", "tp"),
            P("ctx", "tp"),
            P("pipe", "tp", "ctx"),
        ),
        out_specs=P("pipe", "ctx", "tp"),
        check_vma=False,
    )
```

profile of v0, /device:TPU:10, one launch (start us, length us, event | category | flops | bytes accessed | tf_op | source)
XLA Modules:
  0.0 781.1 jit_solution(1275666386259107779)
XLA Ops:
  9.5 2.2 fusion.39
  16.1 29.3 %all_gather.25 = bf16[1024,128]{1,0:T(8,128)(2,1)S(1)} all-gather(bf16[128,128]{1,0:T(8,128)(2,1)S(1)} %constant_dynamic-slice_fusion.2), channel_id=1, replica_groups=mesh['pipe'=2,'ctx'=8,'tp'=2] {'ctx'}, dimensions={0}, use_global_device_ids=true | all-gather | bytes 294912 | tf_op jit(solution)/shard_map/all_gather | solution.py:197
  45.3 33.7 %all_gather.26 = bf16[1024,128]{1,0:T(8,128)(2,1)} all-gather(bf16[128,128]{1,0:T(8,128)(2,1)S(1)} %constant_dynamic-slice_fusion.1), channel_id=1, replica_groups=mesh['pipe'=2,'ctx'=8,'tp'=2] {'ctx'}, dimensions={0}, use_global_device_ids=true | all-gather | bytes 294912 | tf_op jit(solution)/shard_map/all_gather | solution.py:198
  79.1 12.4 %conditional.1 = ((f32[1,16,128]{2,1,0:T(8,128)}, f32[1,16,128,128]{3,2,1,0:T(8,128)S(1)})) conditional(s32[]{:T(128)} %bitcast.31, (f32[1,16,128]{2,1,0:T(8,128)}, f32[1,16,128,128]{3,2,1,0:T(8,128)S(1)}) %tuple.39, (s32[128]{0:T(128)}, bf16[128,4096]{1,0:T(8,128)(2,1)}, s32[]{:T(128)}, bf16[1024,128]{1,0:T(8,128)(2,1)S(1)}, ...), branch_computations={%region_4.5_spmd, %region_5.8_spmd} | conditional | flops 1101668352 | bytes 33129016 | solution.py:189
  79.8 2.3 copy.61
  83.4 1.6 fusion
  85.0 2.6 fusion.10
  87.6 2.6 fusion.2
  90.2 1.3 bitcast_add_fusion
  93.7 61.5 %all-gather.2 = bf16[8,1,32]{2,1,0:T(2,128)(2,1)S(1)} all-gather(bf16[1,1,32]{2,1,0:T(2,128)(2,1)} %get-tuple-element.302), channel_id=2, replica_groups=mesh['pipe'=2,'ctx'=8,'tp'=2] {'ctx'}, dimensions={0}, use_global_device_ids=true | all-gather | bytes 576 | tf_op jit(solution)/shard_map/all_gather | solution.py:21
  156.8 4.5 fusion.31
  161.3 10.7 %while.9 = (s32[]{:T(128)}, f32[1,32,64,128]{3,2,1,0:T(8,128)S(1)}, s32[]{:T(128)}, bf16[8,1,32]{2,1,0:T(2,128)(2,1)S(1)}, bf16[8,1,32,64,128]{4,3,2,1,0:T(8,128)(2,1)}, /*index=5*/s32[]{:T(128)}, s32[]{:T(128)}) while((s32[]{:T(128)}, f32[1,32,64,128]{3,2,1,0:T(8,128)S(1)}, s32[]{:T(128)}, bf16[8,1,32]{2,1,0:T(2,128)(2,1)S(1)}, ...), condition=%wide.region_2.3_spmd.clone, body=%wide.region_1.2_spmd.clone.sunk | while | flops 1310756 | bytes 2621865 | solution.py:34
  161.4 1.3 fusion.87
  162.7 1.3 fusion.87
  165.4 1.3 fusion.87
  172.7 1.8 fusion.37
  174.8 1.5 multiply_reduce_fusion
  176.4 1.8 bitcast_select_fusion.2
  178.5 8.9 %collective-permute-done = bf16[128,2048]{1,0:T(8,128)(2,1)S(1)} collective-permute-done((bf16[128,2048]{1,0:T(8,128)(2,1)S(1)}, bf16[128,2048]{1,0:T(8,128)(2,1)S(1)}, u32[]{:S(2)}, u32[]{:S(2)}) %collective-permute-start) | collective-permute-done | bytes 524320 | tf_op jit(solution)/shard_map/ppermute | solution.py:44
  187.4 542.7 %all-gather.6.cloned.1.call-done = bf16[1,4096,4096]{2,1,0:T(8,128)(2,1)} async-done(((bf16[1,4096,512]{2,1,0:T(8,128)(2,1)}), bf16[1,4096,4096]{2,1,0:T(8,128)(2,1)}) %all-gather.6.cloned.1.call-update) | async-done | bytes 33554448 | tf_op jit(solution)/shard_map/all_gather | solution.py:259
  730.1 16.2 %fusion.22 = bf16[128,4096]{1,0:T(8,128)(2,1)} fusion(bf16[1,4096,4096]{2,1,0:T(8,128)(2,1)} %all-gather.6.cloned.1.call-done, bf16[128,2048]{1,0:T(8,128)(2,1)S(1)} %collective-permute-done, bf16[128,2048]{1,0:T(8,128)(2,1)S(1)} %get-tuple-element.297, pred[]{:T(512)S(6)} %eq.2), kind=kOutput, calls=%fused_computation.27 | convolution fusion | flops 4300210176 | bytes 35651584 | tf_op jit(solution)/shard_map/dot_general | solution.py:257
  746.3 8.9 %reduce-scatter.2.cloned.1.call-done = bf16[128,2048]{1,0:T(8,128)(2,1)} async-done(((bf16[128,4096]{1,0:T(8,128)(2,1)}), bf16[128,2048]{1,0:T(8,128)(2,1)}) %reduce-scatter.2.cloned.1.call-update) | async-done | bytes 524304 | tf_op jit(solution)/shard_map/reduce_scatter | solution.py:262
  757.7 14.7 %collective-permute-done.1 = bf16[128,2048]{1,0:T(8,128)(2,1)S(1)} collective-permute-done((bf16[128,2048]{1,0:T(8,128)(2,1)S(1)}, bf16[128,2048]{1,0:T(8,128)(2,1)S(1)}, u32[]{:S(2)}, u32[]{:S(2)}) %collective-permute-start.1) | collective-permute-done | bytes 524320 | tf_op jit(solution)/shard_map/ppermute | solution.py:50
  772.5 2.1 fusion.62
  (80 shorter events, 22.7 us)
Async XLA Ops:
  6.5 2.6 copy-start
  6.5 7.0 copy-start.10
  6.5 9.5 %copy-start.6 = (bf16[128,256]{1,0:T(8,128)(2,1)S(1)}, bf16[128,256]{1,0:T(8,128)(2,1)}, u32[]{:S(2)}) copy-start(bf16[128,256]{1,0:T(8,128)(2,1)} %param.27) | copy-start | bytes 196612
  6.5 9.5 %copy-start.7 = (bf16[128,256]{1,0:T(8,128)(2,1)S(1)}, bf16[128,256]{1,0:T(8,128)(2,1)}, u32[]{:S(2)}) copy-start(bf16[128,256]{1,0:T(8,128)(2,1)} %param.28) | copy-start | bytes 196612
  6.5 154.8 %all-gather.8.cloned.1.call-start = ((), (), s32[]{:S(2)}) async-start(), calls=%async_computation.3 | async-start | bytes 4718592 | tf_op jit(solution)/shard_map/all_gather | solution.py:21
  9.5 3.1 copy-start.2
  11.7 718.4 %all-gather.6.cloned.1.call-start = ((), (), s32[]{:S(2)}) async-start(), calls=%async_computation.1 | async-start | bytes 37748736 | tf_op jit(solution)/shard_map/all_gather | solution.py:259
  12.5 742.8 %reduce-scatter.2.cloned.1.call-start = ((), (), s32[]{:S(2)}) async-start(), calls=%async_computation.2 | async-start | bytes 1572864 | tf_op jit(solution)/shard_map/reduce_scatter | solution.py:262
  14.1 1.9 copy-start.9
  82.2 2.9 copy-start.4
  156.8 15.2 %copy-start.5 = (bf16[128,256]{1,0:T(8,128)(2,1)S(1)}, bf16[128,256]{1,0:T(8,128)(2,1)}, u32[]{:S(2)}) copy-start(bf16[128,256]{1,0:T(8,128)(2,1)} %param.21) | copy-start | bytes 196612
  161.3 11.3 %copy-start.8 = (f32[32]{0:T(128)S(1)}, f32[32]{0:T(128)}, u32[]{:S(2)}) copy-start(f32[32]{0:T(128)} %dynamic_slice.77) | copy-start | bytes 388
  161.3 15.0 %dynamic-slice-start = ((f32[4096]{0:T(1024)}, s32[]{:T(128)}), f32[2048]{0:T(1024)S(1)}, s32[]{:S(2)}) async-start(f32[4096]{0:T(1024)} %param.25, s32[]{:T(128)} %select_n.88), calls=%async_computation.4 | async-start | bytes 16896 | tf_op jit(solution)/shard_map/dynamic_slice | solution.py:213
  178.2 9.2 %collective-permute-start = (bf16[128,2048]{1,0:T(8,128)(2,1)S(1)}, bf16[128,2048]{1,0:T(8,128)(2,1)S(1)}, u32[]{:S(2)}, u32[]{:S(2)}) collective-permute-start(bf16[128,2048]{1,0:T(8,128)(2,1)S(1)} %get-tuple-element.298), channel_id=1, source_target_pairs={{0,16},{16,0},{1,17},{17,1},{2,18},{18,2},{3,19},{19,3},{4,20},{20... | collective-permute-start | bytes 1572872 | tf_op jit(solution)/shard_map/ppermute | solution.py:44
  730.1 25.1 %copy-start.3 = (bf16[128,2048]{1,0:T(8,128)(2,1)S(1)}, bf16[128,2048]{1,0:T(8,128)(2,1)}, u32[]{:S(2)}) copy-start(bf16[128,2048]{1,0:T(8,128)(2,1)} %param.17) | copy-start | bytes 1572868
  730.1 44.4 %copy-start.1 = (bf16[128,4096]{1,0:T(8,128)(2,1)S(1)}, bf16[128,4096]{1,0:T(8,128)(2,1)}, u32[]{:S(2)}) copy-start(bf16[128,4096]{1,0:T(8,128)(2,1)} %param.18) | copy-start | bytes 3145732
  756.4 16.0 %collective-permute-start.1 = (bf16[128,2048]{1,0:T(8,128)(2,1)S(1)}, bf16[128,2048]{1,0:T(8,128)(2,1)S(1)}, u32[]{:S(2)}, u32[]{:S(2)}) collective-permute-start(bf16[128,2048]{1,0:T(8,128)(2,1)S(1)} %fusion.44), channel_id=1, source_target_pairs={{0,16},{1,17},{2,18},{3,19},{4,20},{5,21},{6,22},{7,23},{8,24},{9,... | collective-permute-start | bytes 1572872 | tf_op jit(solution)/shard_map/ppermute | solution.py:50
Sparse Core Ops, SparseCore 0:
  11.8 79.6 all-gather.7
  93.0 637.0 all-gather.5
  746.5 8.7 reduce-scatter.1
where the time goes:
time: 783 us; the launch traced here: 781 us
  waiting for transfers between devices  576 us (74%)
  blocking collectives  124 us (16%)
  matrix products  30.4 us (4%)
  other arithmetic  23.5 us (3%)
  between operations  14 us (2%)
  local copies, waits for them, and re-layouts  10.6 us (1%)
    all_gather x1, waiting for transfers between devices, per_device(): lax.all_gather(out_weights, 'ctx', axis=2, tiled=True)[0]  543 us
    all_gather x1, blocking collectives, entering_2(): lax.all_gather(part.astype(kind), axis)  61.5 us
    all_gather x1, blocking collectives, attention(): value_piece = lax.all_gather(values, 'ctx', axis=0, tiled=True)  33.7 us
    all_gather x1, blocking collectives, attention(): key_piece = lax.all_gather(keys, 'ctx', axis=0, tiled=True)  29.3 us
    dot_general x1, matrix products, per_device(): jnp.dot(mixed_rows, lax.all_gather(out_weights, 'ctx', axis=2, tiled=True...  16.2 us
  transfers between devices with their start and end apart: 5, of which 4 were waited for; matrix products, arithmetic and copies ran while one was open for 5% of the time, Pallas kernels for 0%

commit v1 on v0

v1 whole, which is shorter than its diff:
```python
import math

import jax
import jax.numpy as jnp
from jax import lax
from jax.sharding import PartitionSpec as P

MHEAD_DIM = 64
STATE = 128
HEAD_DIM = 128


exact_mode = lax.Precision.HIGHEST
norm_eps = 1e-05


def from_partner(block, axis, distance):
    count = lax.axis_size(axis)
    route = []
    for low in range(count):
        high = low | 1 << distance
        if high != low and high < count:
            route += [(low, high), (high, low)]
    return lax.ppermute(block, axis, route)


def shifted(x, axis, by):
    peers = lax.axis_size(axis)
    pairs = [(i, i + by) for i in range(peers) if 0 <= i + by < peers]
    return lax.ppermute(x, axis, pairs)


def expand(per_head, width):
    return jnp.repeat(per_head, width, axis=1)


def mamba_local(x, b, c, step, rate, skip):
    rows, heads = step.shape
    log_decay = -step * rate[None, :]
    tri = jnp.arange(rows)[:, None] >= jnp.arange(rows)[None, :]
    running = jnp.dot(tri.astype(jnp.float32), log_decay, precision=exact_mode)
    cross = jnp.einsum("tn,sn->ts", c, b, preferred_element_type=jnp.float32)
    spread = running.T[:, :, None] - running.T[:, None, :]
    decay = jnp.exp(jnp.where(tri[None], spread, -jnp.inf))
    mixing = (cross[None] * decay * step.T[:, None, :]).astype(jnp.bfloat16)
    heads_x = x.reshape(rows, heads, MHEAD_DIM)
    within = jnp.einsum("hts,shp->thp", mixing, heads_x, preferred_element_type=jnp.float32)
    xf = x.astype(jnp.float32)
    within = within.reshape(rows, -1) + xf * jnp.repeat(skip, MHEAD_DIM)[None, :]
    tail = jnp.exp(running[-1:] - running) * step
    weighted = (xf * expand(tail, MHEAD_DIM)).astype(jnp.bfloat16)
    state = jnp.einsum("sp,sn->np", weighted, b, preferred_element_type=jnp.float32)
    return running, within, state


def entering_state(running, state):
    peers, position = lax.axis_size("ctx"), lax.axis_index("ctx")
    last = running[-1]
    logs = lax.all_gather(last, "ctx")
    have, total = state, last
    reach = 1
    while reach < peers:
        pairs = [(i, i + reach) for i in range(peers - reach)]
        got = lax.ppermute(have.astype(jnp.bfloat16), "ctx", pairs).astype(jnp.float32)
        have = have + jnp.exp(jnp.repeat(total, MHEAD_DIM))[None, :] * got
        span = jnp.arange(peers)
        inside = (span <= position) & (span > position - 2 * reach)
        total = jnp.sum(jnp.where(inside[:, None], logs, 0.0), axis=0)
        reach *= 2
    pairs = [(i, i + 1) for i in range(peers - 1)]
    return lax.ppermute(have.astype(jnp.bfloat16), "ctx", pairs)


def mamba_mixer(x, gate, b, c, step, rate, skip, gains):
    running, within, state = mamba_local(x, b, c, step, rate, skip)
    entering = entering_state(running, state)
    carried = jnp.dot(c, entering, preferred_element_type=jnp.float32)
    y = within + carried * expand(jnp.exp(running), MHEAD_DIM)
    gated = y * jax.nn.silu(gate.astype(jnp.float32))
    per_group = gated.reshape(gated.shape[0], b.shape[1] // STATE, -1)
    meansq = jnp.mean(per_group * per_group, axis=-1, keepdims=True)
    scaled = (per_group * lax.rsqrt(meansq + norm_eps)).reshape(gated.shape)
    return (scaled * gains[None, :]).astype(jnp.bfloat16)


def attention(queries, keys, values, ctx_rank):
    rows = queries.shape[0]
    both = lax.all_gather(jnp.concatenate([keys, values], axis=1), "ctx", axis=0, tiled=True)
    k, v = both[:, :HEAD_DIM], both[:, HEAD_DIM:]
    heads = queries.shape[1] // HEAD_DIM
    q = queries.reshape(rows, heads, HEAD_DIM)
    scores = jnp.einsum("qjd,kd->jqk", q, k, preferred_element_type=jnp.float32)
    scores = scores * (1.0 / math.sqrt(HEAD_DIM))
    position = ctx_rank * rows + jnp.arange(rows)
    allowed = jnp.arange(k.shape[0])[None, :] <= position[:, None]
    scores = jnp.where(allowed[None], scores, -jnp.inf)
    weights = jnp.exp(scores - jnp.max(scores, axis=-1, keepdims=True))
    total = jnp.sum(weights, axis=-1)
    mixed = jnp.einsum("jqk,kd->qjd", weights.astype(jnp.bfloat16), v, preferred_element_type=jnp.float32)
    return (mixed / total.T[:, :, None]).reshape(rows, -1).astype(jnp.bfloat16)


def take_half(array, axis_dim, section):
    width = array.shape[axis_dim] // 2
    return lax.dynamic_slice_in_dim(array, section * width, width, axis_dim)


def per_device(
    resid_in,
    ssm_input,
    ssm_gate,
    ssm_in_b,
    ssm_out_c,
    step_size,
    decay_rate,
    skip_gain,
    norm_gain,
    queries,
    keys,
    values,
    out_weights,
):
    section = lax.axis_index("pipe")
    ctx_rank = lax.axis_index("ctx")
    mamba_part = mamba_mixer(
        take_half(ssm_input, 1, section),
        take_half(ssm_gate, 1, section),
        take_half(ssm_in_b, 1, section),
        take_half(ssm_out_c, 1, section),
        take_half(step_size, 1, section),
        take_half(decay_rate, 0, section),
        take_half(skip_gain, 0, section),
        take_half(norm_gain, 0, section),
    )
    attn_part = attention(
        take_half(queries, 1, section),
        take_half(keys, 1, section),
        take_half(values, 1, section),
        ctx_rank,
    )
    outgoing = jnp.where(section == 0, attn_part, mamba_part)
    kept_half = jnp.where(section == 0, mamba_part, attn_part)
    incoming = from_partner(outgoing, "pipe", 0)
    mixed_rows = jnp.where(
        section == 0,
        jnp.concatenate([kept_half, incoming], axis=1),
        jnp.concatenate([incoming, kept_half], axis=1),
    )
    peers = lax.axis_size("ctx")
    rows = mixed_rows.shape[0]
    gathered = lax.all_gather(mixed_rows, "ctx", axis=0, tiled=True)
    partial = jnp.dot(gathered, out_weights[0], preferred_element_type=jnp.float32).astype(jnp.bfloat16)
    pieces = lax.all_to_all(partial.reshape(peers, rows, -1), "ctx", 0, 0)
    whole = pieces.transpose(1, 0, 2).reshape(rows, -1)
    projected = lax.psum_scatter(whole, "tp", scatter_dimension=1, tiled=True).astype(jnp.float32)
    own_section = (resid_in.astype(jnp.float32) + projected).astype(jnp.bfloat16)
    received = shifted(own_section, "pipe", 1)
    second_section = (received.astype(jnp.float32) + projected).astype(jnp.bfloat16)
    return jnp.where(section == 0, own_section, second_section)[None]


def solution(mesh):
    return jax.shard_map(
        per_device,
        mesh=mesh,
        in_specs=(
            P("ctx", "tp"),
            P("ctx", "tp"),
            P("ctx", "tp"),
            P("ctx", "tp"),
            P("ctx", "tp"),
            P("ctx", "tp"),
            P("tp"),
            P("tp"),
            P("tp"),
            P("ctx", "tp"),
            P("ctx", "tp"),
            P("ctx", "tp"),
            P("pipe", "tp", "ctx"),
        ),
        out_specs=P("pipe", "ctx", "tp"),
        check_vma=False,
    )
```

time: 783 us -> 332 us (0.42)
  waiting for transfers between devices: 576 us -> 180 us
  blocking collectives: 124 us -> 86.6 us
  other arithmetic: 23.5 us -> 9.93 us
  matrix products: 30.4 us -> 20.3 us
  starting transfers between devices: 1.79 us -> 11.4 us
    all_gather x2 -> x1, waiting for transfers between devices: 543 us -> 124 us  [per_device(): gathered = lax.all_gather(mixed_rows, 'ctx', axis=0, tiled=True)]
    all_gather x3 -> x2, blocking collectives: 124 us -> 56.8 us  [the longest x1 33.8 us: attention(): lax.all_gather(jnp.concatenate([keys, values], axis=1), 'ctx', axis=0, ti...]
    all_to_all x0 -> x1, blocking collectives: none -> 29.9 us  [per_device(): pieces = lax.all_to_all(partial.reshape(peers, rows, -1), 'ctx', 0, 0)]
    ppermute x0 -> x4, waiting for transfers between devices: none -> 24.7 us  [the longest x3 23.7 us: entering_state(): lax.ppermute(have.astype(jnp.bfloat16), 'ctx', pairs).astype(jnp.float32)]
    dot_general x8, matrix products: 30.4 us -> 20.3 us  [the longest x1 9.05 us: per_device(): jnp.dot(gathered, out_weights[0], preferred_element_type=jnp.float32)]
    ppermute x0 -> x4, starting transfers between devices: none -> 9.24 us  [the longest x3 6.65 us: entering_state(): lax.ppermute(have.astype(jnp.bfloat16), 'ctx', pairs).astype(jnp.float32)]
    select_n x8 -> x1, other arithmetic: 10.4 us -> 1.3 us  [per_device(): jnp.where(section == 0, jnp.concatenate([kept_half, incoming], axis=1), j...]
  transfers between devices with their start and end apart: 5 -> 8, of which waited for: 4 -> 7; matrix products, arithmetic and copies ran while one was open for 5% -> 4% of each run, Pallas kernels for 0% -> 0%
where the time goes in v1:
time: 332 us; the launch traced here: 330 us
  waiting for transfers between devices  180 us (54%)
  blocking collectives  86.6 us (26%)
  matrix products  20.3 us (6%)
  between operations  13.7 us (4%)
  starting transfers between devices  11.4 us (3%)
  other arithmetic  9.93 us (3%)
  local copies, waits for them, and re-layouts  7.92 us (2%)
    all_gather x1, waiting for transfers between devices, per_device(): gathered = lax.all_gather(mixed_rows, 'ctx', axis=0, tiled=True)  124 us
    all_gather x1, blocking collectives, attention(): lax.all_gather(jnp.concatenate([keys, values], axis=1), 'ctx', axis=0, ti...  33.8 us
    all_to_all x1, blocking collectives, per_device(): pieces = lax.all_to_all(partial.reshape(peers, rows, -1), 'ctx', 0, 0)  29.9 us
    ppermute x3, waiting for transfers between devices, entering_state(): lax.ppermute(have.astype(jnp.bfloat16), 'ctx', pairs).astype(jnp.float32)  23.7 us
    all_gather x1, blocking collectives, entering_state(): logs = lax.all_gather(last, 'ctx')  23 us
    ppermute x1, waiting for transfers between devices, shifted(): return lax.ppermute(x, axis, pairs)  14.7 us
    dot_general x1, matrix products, per_device(): jnp.dot(gathered, out_weights[0], preferred_element_type=jnp.float32)  9.05 us
    ppermute x1, waiting for transfers between devices, from_partner(): return lax.ppermute(block, axis, route)  8.61 us
  transfers between devices with their start and end apart: 8, of which 7 were waited for; matrix products, arithmetic and copies ran while one was open for 4% of the time, Pallas kernels for 0%

profile of v1, /device:TPU:10, one launch (start us, length us, event | category | flops | bytes accessed | tf_op | source)
XLA Modules:
  0.0 330.3 jit_solution(418685633120076415)
XLA Ops:
  9.7 1.3 constant_dynamic-slice_fusion
  12.1 3.4 %collective-permute-start = (bf16[128,2048]{1,0:T(8,128)(2,1)}, bf16[128,2048]{1,0:T(8,128)(2,1)S(1)}, u32[]{:S(2)}, u32[]{:S(2)}) collective-permute-start(bf16[128,2048]{1,0:T(8,128)(2,1)} %get-tuple-element.14), channel_id=1, source_target_pairs={{0,2},{2,4},{4,6},{6,8},{8,10},{10,12},{12,14},{1,3},{3,5},{5,7},{... | collective-permute-start | bytes 1572872 | tf_op jit(solution)/shard_map/ppermute | solution.py:64
  16.0 23.0 %all-gather = f32[8,1,32]{2,1,0:T(1,128)S(1)} all-gather(f32[1,1,32]{2,1,0:T(1,128)S(1)} %bitcast.66), channel_id=1, replica_groups=mesh['pipe'=2,'ctx'=8,'tp'=2] {'ctx'}, dimensions={0}, use_global_device_ids=true | all-gather | bytes 1152 | tf_op jit(solution)/shard_map/all_gather | solution.py:59
  39.1 33.8 %all_gather.10 = bf16[1024,256]{1,0:T(8,128)(2,1)} all-gather(bf16[128,256]{1,0:T(8,128)(2,1)S(1)} %pad_maximum_fusion), channel_id=1, replica_groups=mesh['pipe'=2,'ctx'=8,'tp'=2] {'ctx'}, dimensions={0}, use_global_device_ids=true | all-gather | bytes 589824 | tf_op jit(solution)/shard_map/all_gather | solution.py:88
  73.8 1.9 collective-permute-start.1
  76.1 2.2 fusion.2
  78.4 13.2 %collective-permute-done.1 = bf16[128,2048]{1,0:T(8,128)(2,1)S(1)} collective-permute-done((bf16[128,2048]{1,0:T(8,128)(2,1)}, bf16[128,2048]{1,0:T(8,128)(2,1)S(1)}, u32[]{:S(2)}, u32[]{:S(2)}) %collective-permute-start.1) | collective-permute-done | bytes 524320 | tf_op jit(solution)/shard_map/ppermute | solution.py:64
  91.8 1.3 collective-permute-start.2
  93.1 1.7 fusion
  94.9 10.5 %collective-permute-done.2 = bf16[128,2048]{1,0:T(8,128)(2,1)S(1)} collective-permute-done((bf16[128,2048]{1,0:T(8,128)(2,1)S(1)}, bf16[128,2048]{1,0:T(8,128)(2,1)S(1)}, u32[]{:S(2)}, u32[]{:S(2)}) %collective-permute-start.2) | collective-permute-done | bytes 524320 | tf_op jit(solution)/shard_map/ppermute | solution.py:64
  106.5 2.6 collective-permute-start.3
  109.2 2.1 divide_convert_fusion
  113.0 2.9 fusion.16
  116.0 1.6 copy.33
  118.8 1.9 multiply_reduce_fusion
  121.7 8.6 %collective-permute-done.4 = bf16[128,2048]{1,0:T(8,128)(2,1)S(1)} collective-permute-done((bf16[128,2048]{1,0:T(8,128)(2,1)S(1)}, bf16[128,2048]{1,0:T(8,128)(2,1)S(1)}, u32[]{:S(2)}, u32[]{:S(2)}) %collective-permute-start.4) | collective-permute-done | bytes 524320 | tf_op jit(solution)/shard_map/ppermute | solution.py:24
  130.3 1.3 maximum_select_fusion
  131.8 124.0 %all-gather.3.cloned.1.call-done = bf16[1024,4096]{1,0:T(8,128)(2,1)} async-done(((bf16[128,4096]{1,0:T(8,128)(2,1)}), bf16[1024,4096]{1,0:T(8,128)(2,1)}) %all-gather.3.cloned.1.call-update) | async-done | bytes 8388624 | tf_op jit(solution)/shard_map/all_gather | solution.py:151
  255.8 9.0 %fusion.10 = bf16[1024,512]{1,0:T(8,128)(2,1)S(1)} fusion(bf16[1024,4096]{1,0:T(8,128)(2,1)} %all-gather.3.cloned.1.call-done, bf16[1,4096,512]{2,1,0:T(8,128)(2,1)} %param.25), kind=kOutput, calls=%fused_computation.13 | convolution fusion | flops 4295491584 | bytes 13631488 | tf_op jit(solution)/shard_map/dot_general | solution.py:152
  264.9 29.9 %all_to_all.5 = bf16[8,128,512]{2,1,0:T(8,128)(2,1)S(1)} all-to-all(bf16[8,128,512]{2,1,0:T(8,128)(2,1)S(1)} %bitcast.60), channel_id=1, replica_groups=mesh['pipe'=2,'ctx'=8,'tp'=2] {'ctx'}, dimensions={0} | all-to-all | bytes 2097152 | tf_op jit(solution)/shard_map/all_to_all | solution.py:153
  295.8 8.4 %reduce-scatter.2.cloned.1.call-done = bf16[128,2048]{1,0:T(8,128)(2,1)} async-done(((bf16[128,4096]{1,0:T(8,128)(2,1)}), bf16[128,2048]{1,0:T(8,128)(2,1)}) %reduce-scatter.2.cloned.1.call-update) | async-done | bytes 524304 | tf_op jit(solution)/shard_map/reduce_scatter | solution.py:155
  305.4 1.3 collective-permute-start.5
  306.7 14.7 %collective-permute-done.5 = bf16[128,2048]{1,0:T(8,128)(2,1)S(1)} collective-permute-done((bf16[128,2048]{1,0:T(8,128)(2,1)S(1)}, bf16[128,2048]{1,0:T(8,128)(2,1)S(1)}, u32[]{:S(2)}, u32[]{:S(2)}) %collective-permute-start.5) | collective-permute-done | bytes 524320 | tf_op jit(solution)/shard_map/ppermute | solution.py:30
  321.4 2.1 fusion.34
  (62 shorter events, 14.0 us)
Async XLA Ops:
  6.5 4.4 %copy-start = (bf16[128,256]{1,0:T(8,128)(2,1)S(1)}, bf16[128,256]{1,0:T(8,128)(2,1)}, u32[]{:S(2)}) copy-start(bf16[128,256]{1,0:T(8,128)(2,1)} %param.16) | copy-start | bytes 196612
  6.5 32.4 %copy-start.3 = (bf16[128,256]{1,0:T(8,128)(2,1)S(1)}, bf16[128,256]{1,0:T(8,128)(2,1)}, u32[]{:S(2)}) copy-start(bf16[128,256]{1,0:T(8,128)(2,1)} %param.24) | copy-start | bytes 196612
  6.5 32.4 %copy-start.4 = (bf16[128,256]{1,0:T(8,128)(2,1)S(1)}, bf16[128,256]{1,0:T(8,128)(2,1)}, u32[]{:S(2)}) copy-start(bf16[128,256]{1,0:T(8,128)(2,1)} %param.23) | copy-start | bytes 196612
  6.5 249.3 %all-gather.3.cloned.1.call-start = ((), (), s32[]{:S(2)}) async-start(), calls=%async_computation.2 | async-start | bytes 9437184 | tf_op jit(solution)/shard_map/all_gather | solution.py:151
  12.1 60.8 %collective-permute-start = (bf16[128,2048]{1,0:T(8,128)(2,1)}, bf16[128,2048]{1,0:T(8,128)(2,1)S(1)}, u32[]{:S(2)}, u32[]{:S(2)}) collective-permute-start(bf16[128,2048]{1,0:T(8,128)(2,1)} %get-tuple-element.14), channel_id=1, source_target_pairs={{0,2},{2,4},{4,6},{6,8},{8,10},{10,12},{12,14},{1,3},{3,5},{5,7},{... | collective-permute-start | bytes 1572872 | tf_op jit(solution)/shard_map/ppermute | solution.py:64
  73.8 17.7 %collective-permute-start.1 = (bf16[128,2048]{1,0:T(8,128)(2,1)}, bf16[128,2048]{1,0:T(8,128)(2,1)S(1)}, u32[]{:S(2)}, u32[]{:S(2)}) collective-permute-start(bf16[128,2048]{1,0:T(8,128)(2,1)} %fusion.32), channel_id=1, source_target_pairs={{0,4},{2,6},{4,8},{6,10},{8,12},{10,14},{1,5},{3,7},{5,9},{7,11},{... | collective-permute-start | bytes 1572872 | tf_op jit(solution)/shard_map/ppermute | solution.py:64
  78.4 30.8 %copy-start.1 = (bf16[1024,256]{1,0:T(8,128)(2,1)S(1)}, bf16[1024,256]{1,0:T(8,128)(2,1)}, u32[]{:S(2)}) copy-start(bf16[1024,256]{1,0:T(8,128)(2,1)} %all_gather.10) | copy-start | bytes 1572868
  91.8 13.6 %collective-permute-start.2 = (bf16[128,2048]{1,0:T(8,128)(2,1)S(1)}, bf16[128,2048]{1,0:T(8,128)(2,1)S(1)}, u32[]{:S(2)}, u32[]{:S(2)}) collective-permute-start(bf16[128,2048]{1,0:T(8,128)(2,1)S(1)} %fusion.37), channel_id=1, source_target_pairs={{0,8},{2,10},{4,12},{6,14},{1,9},{3,11},{5,13},{7,15},{16,24},{18,... | collective-permute-start | bytes 1572872 | tf_op jit(solution)/shard_map/ppermute | solution.py:64
  106.5 12.3 %collective-permute-start.3 = (bf16[128,2048]{1,0:T(8,128)(2,1)}, bf16[128,2048]{1,0:T(8,128)(2,1)}, u32[]{:S(2)}, u32[]{:S(2)}) collective-permute-start(bf16[128,2048]{1,0:T(8,128)(2,1)} %add_convert_fusion), channel_id=1, source_target_pairs={{0,2},{2,4},{4,6},{6,8},{8,10},{10,12},{12,14},{1,3},{3,5},{5,7},{... | collective-permute-start | bytes 1572872 | tf_op jit(solution)/shard_map/ppermute | solution.py:71
  109.1 3.8 %copy-start.5 = (bf16[128,256]{1,0:T(8,128)(2,1)S(1)}, bf16[128,256]{1,0:T(8,128)(2,1)}, u32[]{:S(2)}) copy-start(bf16[128,256]{1,0:T(8,128)(2,1)} %param.17) | copy-start | bytes 196612
  111.2 6.3 %copy-start.6 = (f32[64]{0:T(128)S(1)}, f32[64]{0:T(128)}, u32[]{:S(2)}) copy-start(f32[64]{0:T(128)} %param.20) | copy-start | bytes 772
  112.2 8.5 %dynamic-slice-start = ((f32[4096]{0:T(1024)}, s32[]{:T(128)}), f32[2048]{0:T(1024)S(1)}, s32[]{:S(2)}) async-start(f32[4096]{0:T(1024)} %param.21, s32[]{:T(128)} %select_n.58), calls=%async_computation.4 | async-start | bytes 16896 | tf_op jit(solution)/shard_map/dynamic_slice | solution.py:105
  121.0 9.2 %collective-permute-start.4 = (bf16[128,2048]{1,0:T(8,128)(2,1)S(1)}, bf16[128,2048]{1,0:T(8,128)(2,1)S(1)}, u32[]{:S(2)}, u32[]{:S(2)}) collective-permute-start(bf16[128,2048]{1,0:T(8,128)(2,1)S(1)} %get-tuple-element.8), channel_id=1, source_target_pairs={{0,16},{16,0},{1,17},{17,1},{2,18},{18,2},{3,19},{19,3},{4,20},{20... | collective-permute-start | bytes 1572872 | tf_op jit(solution)/shard_map/ppermute | solution.py:24
  131.6 172.6 %copy-start.2 = (bf16[128,2048]{1,0:T(8,128)(2,1)S(1)}, bf16[128,2048]{1,0:T(8,128)(2,1)}, u32[]{:S(2)}) copy-start(bf16[128,2048]{1,0:T(8,128)(2,1)} %param.13) | copy-start | bytes 1572868
  131.6 172.6 %reduce-scatter.2.cloned.1.call-start = ((), (), s32[]{:S(2)}) async-start(), calls=%async_computation.3 | async-start | bytes 1572864 | tf_op jit(solution)/shard_map/reduce_scatter | solution.py:155
  305.4 16.0 %collective-permute-start.5 = (bf16[128,2048]{1,0:T(8,128)(2,1)S(1)}, bf16[128,2048]{1,0:T(8,128)(2,1)S(1)}, u32[]{:S(2)}, u32[]{:S(2)}) collective-permute-start(bf16[128,2048]{1,0:T(8,128)(2,1)S(1)} %fusion.22), channel_id=1, source_target_pairs={{0,16},{1,17},{2,18},{3,19},{4,20},{5,21},{6,22},{7,23},{8,24},{9,... | collective-permute-start | bytes 1572872 | tf_op jit(solution)/shard_map/ppermute | solution.py:30
Sparse Core Ops, SparseCore 0:
  131.7 124.0 all-gather.2
  296.0 8.1 reduce-scatter.1

commit v2 on v1

--- a/solution.py
+++ b/solution.py
@@ -1,8 +1,11 @@
+import functools
 import math
 
 import jax
 import jax.numpy as jnp
 from jax import lax
+from jax.experimental import pallas as pl
+from jax.experimental.pallas import tpu as pltpu
 from jax.sharding import PartitionSpec as P
 
 MHEAD_DIM = 64
@@ -10,24 +13,288 @@
 HEAD_DIM = 128
 
 
+MESH = pl.DeviceIdType.MESH
 exact_mode = lax.Precision.HIGHEST
 norm_eps = 1e-05
 
 
-def from_partner(block, axis, distance):
-    count = lax.axis_size(axis)
-    route = []
-    for low in range(count):
-        high = low | 1 << distance
-        if high != low and high < count:
-            route += [(low, high), (high, low)]
-    return lax.ppermute(block, axis, route)
-
-
-def shifted(x, axis, by):
-    peers = lax.axis_size(axis)
-    pairs = [(i, i + by) for i in range(peers) if 0 <= i + by < peers]
-    return lax.ppermute(x, axis, pairs)
+def share_kernel(n, kv_ref, log_ref, kv_all, log_all, kv_send, kv_recv, log_send, log_recv):
+    pipe, me, tp = (lax.axis_index(a) for a in ("pipe", "ctx", "tp"))
+    barrier = pltpu.get_barrier_semaphore()
+    for k in range(1, n):
+        peer = lax.rem(me + k, n)
+        pl.semaphore_signal(barrier, inc=1, device_id=(pipe, peer, tp), device_id_type=MESH)
+    kv_all[me] = kv_ref[...]
+    log_all[me] = log_ref[...]
+    pl.semaphore_wait(barrier, n - 1)
+
+    def copies(k, slot):
+        target = (pipe, lax.rem(me + k, n), tp)
+        return (
+            pltpu.make_async_remote_copy(
+                kv_ref, kv_all.at[slot], kv_send.at[k], kv_recv.at[slot],
+                device_id=target, device_id_type=MESH,
+            ),
+            pltpu.make_async_remote_copy(
+                log_ref, log_all.at[slot], log_send.at[k], log_recv.at[slot],
+                device_id=target, device_id_type=MESH,
+            ),
+        )
+
+    for k in range(1, n):
+        for copy in copies(k, me):
+            copy.start()
+    for k in range(1, n):
+        for copy in copies(k, lax.rem(me + k, n)):
+            copy.wait_recv()
+        for copy in copies(k, me):
+            copy.wait_send()
+
+
+def share(kv, last, n):
+    vmem = pl.BlockSpec(memory_space=pltpu.VMEM)
+    logs = jnp.broadcast_to(last[None, :], (8, last.shape[0]))
+    logs = jnp.pad(logs, ((0, 0), (0, -last.shape[0] % 128)))
+    kv_all, log_all = pl.pallas_call(
+        functools.partial(share_kernel, n),
+        out_shape=(
+            jax.ShapeDtypeStruct((n, *kv.shape), kv.dtype),
+            jax.ShapeDtypeStruct((n, *logs.shape), logs.dtype),
+        ),
+        in_specs=[vmem] * 2,
+        out_specs=(vmem, vmem),
+        scratch_shapes=[pltpu.SemaphoreType.DMA((n,))] * 4,
+        compiler_params=pltpu.CompilerParams(
+            collective_id=0, has_side_effects=True, vmem_limit_bytes=32 * 2**20
+        ),
+        name="share",
+    )(kv, logs)
+    return kv_all.reshape(-1, kv.shape[1]), log_all[:, 0, : last.shape[0]]
+
+
+def project_kernel(
+    n, kept, outgoing, weights, resid, out,
+    rows, staged, parts, first,
+    row_recv, up_send, down_send, side_send, pipe_send, part_send, part_recv, first_send, first_recv,
+):
+    pipe, me, tp = (lax.axis_index(a) for a in ("pipe", "ctx", "tp"))
+    line, half_n = n // 2, n // 2
+    pos = me // 2
+    side = me + 1 - 2 * lax.rem(me, 2)
+    owner_tp, own_chunk = me // half_n, lax.rem(me, half_n)
+    other = 1 - pipe
+    width = weights.shape[1]
+    depth = kept.shape[1]
+
+    barrier = pltpu.get_barrier_semaphore()
+    here = me * 2 + tp
+    for k in range(1, 2 * n):
+        there = lax.rem(here + k, 2 * n)
+        pl.semaphore_signal(
+            barrier, inc=1, device_id=(pipe, there // 2, lax.rem(there, 2)), device_id_type=MESH
+        )
+    pl.semaphore_signal(barrier, inc=1, device_id=(other, me, tp), device_id_type=MESH)
+    rows[me, pipe] = kept[...]
+    pl.semaphore_wait(barrier, 2 * n)
+
+    def hop(c, h, sem, ctx):
+        return pltpu.make_async_remote_copy(
+            rows.at[c, h], rows.at[c, h], sem.at[c, h], row_recv.at[c, h],
+            device_id=(pipe, ctx, tp), device_id_type=MESH,
+        )
+
+    def cross(h):
+        return pltpu.make_async_remote_copy(
+            outgoing, rows.at[me, h], pipe_send, row_recv.at[me, h],
+            device_id=(other, me, tp), device_id_type=MESH,
+        )
+
+    up, down = jnp.minimum(me + 2, n - 1), jnp.maximum(me - 2, 0)
+    can_up, can_down = pos + 1 < line, pos > 0
+
+    def part_copy(c):
+        return pltpu.make_async_remote_copy(
+            staged.at[c], parts.at[own_chunk, tp], part_send.at[c], part_recv.at[own_chunk, tp],
+            device_id=(pipe, c, owner_tp), device_id_type=MESH,
+        )
+
+    def is_mine(c):
+        return (c == me) & (owner_tp == tp)
+
+    cross(pipe).start()
+
+    def forward(s, act):
+        @pl.when(s == 0)
+        def _():
+            for turn in range(2):
+                h = pipe if turn == 0 else other
+                if turn == 1:
+                    act(cross(other), None)
+
+                @pl.when(can_up)
+                def _():
+                    act(None, hop(me, h, up_send, up))
+
+                @pl.when(can_down)
+                def _():
+                    act(None, hop(me, h, down_send, down))
+
+                act(None, hop(me, h, side_send, side))
+
+        @pl.when((s > 0) & (s < line))
+        def _():
+            for turn in range(2):
+                h = pipe if turn == 0 else other
+                below, above = me - 2 * s, me + 2 * s
+
+                @pl.when(below >= 0)
+                def _():
+                    act(hop(below, h, up_send, up), None)
+
+                    @pl.when(can_up)
+                    def _():
+                        act(None, hop(below, h, up_send, up))
+
+                    act(None, hop(below, h, side_send, side))
+
+                @pl.when(above < n)
+                def _():
+                    act(hop(above, h, down_send, down), None)
+
+                    @pl.when(can_down)
+                    def _():
+                        act(None, hop(above, h, down_send, down))
+
+                    act(None, hop(above, h, side_send, side))
+
+    def go(arrived, leaving):
+        if arrived is not None:
+            arrived.wait_recv()
+        if leaving is not None:
+            leaving.start()
+
+    def drain(arrived, leaving):
+        if leaving is not None:
+            leaving.wait_send()
+
+    def multiply(c):
+        total = jnp.dot(rows[c, 0], weights[:depth], preferred_element_type=jnp.float32)
+        total += jnp.dot(rows[c, 1], weights[depth:], preferred_element_type=jnp.float32)
+        piece = total.astype(jnp.bfloat16)
+
+        @pl.when(is_mine(c))
+        def _():
+            parts[own_chunk, tp] = piece
+
+        @pl.when(jnp.logical_not(is_mine(c)))
+        def _():
+            staged[c] = piece
+            part_copy(c).start()
+
+    def turn(s, carry):
+        forward(s, go)
+
+        def block(k, carry):
+            late = k // 2
+            dist = s - late
+            centre = me + late * (side - me)
+            c = centre + (2 * lax.rem(k, 2) - 1) * 2 * dist
+            ok = (dist >= 0) & (dist < line) & (c >= 0) & (c < n)
+            ok = ok & ((dist > 0) | (lax.rem(k, 2) == 0))
+
+            @pl.when(ok)
+            def _():
+                @pl.when(late == 1)
+                def _():
+                    for h in range(2):
+                        hop(c, h, side_send, side).wait_recv()
+
+                multiply(c)
+
+            return carry
+
+        return lax.fori_loop(0, 4, block, carry)
+
+    lax.fori_loop(0, line + 1, turn, 0)
+
+    def first_copy(q):
+        return pltpu.make_async_remote_copy(
+            first.at[q], first.at[q], first_send.at[q], first_recv.at[q],
+            device_id=(other, me, tp), device_id_type=MESH,
+        )
+
+    for q in range(half_n):
+        source = tp * half_n + q
+        for t in range(2):
+
+            @pl.when(jnp.logical_not((source == me) & (tp == t)))
+            def _():
+                pltpu.make_async_remote_copy(
+                    parts.at[q, t], parts.at[q, t], part_send.at[0], part_recv.at[q, t],
+                    device_id=(pipe, side, tp), device_id_type=MESH,
+                ).wait_recv()
+
+        total = parts[q, 0].astype(jnp.float32) + parts[q, 1].astype(jnp.float32)
+        columns = slice(q * width, (q + 1) * width)
+
+        @pl.when(pipe == 0)
+        def _():
+            done = (resid[:, columns].astype(jnp.float32) + total).astype(jnp.bfloat16)
+            first[q] = done
+            out[:, columns] = done
+            first_copy(q).start()
+
+        @pl.when(pipe == 1)
+        def _():
+            first_copy(q).wait_recv()
+            out[:, columns] = (first[q].astype(jnp.float32) + total).astype(jnp.bfloat16)
+
+    cross(pipe).wait_send()
+
+    def finish(s, carry):
+        forward(s, drain)
+        return carry
+
+    lax.fori_loop(0, line, finish, 0)
+
+    def sent(c, carry):
+        @pl.when(jnp.logical_not(is_mine(c)))
+        def _():
+            part_copy(c).wait_send()
+
+        return carry
+
+    lax.fori_loop(0, n, sent, 0)
+
+    @pl.when(pipe == 0)
+    def _():
+        for q in range(half_n):
+            first_copy(q).wait_send()
+
+
+def project(kept, outgoing, weights, resid, n):
+    vmem = pl.BlockSpec(memory_space=pltpu.VMEM)
+    count, depth = kept.shape
+    width = weights.shape[1]
+    dma = pltpu.SemaphoreType.DMA
+    return pl.pallas_call(
+        functools.partial(project_kernel, n),
+        out_shape=jax.ShapeDtypeStruct(resid.shape, jnp.bfloat16),
+        in_specs=[vmem] * 4,
+        out_specs=vmem,
+        scratch_shapes=[
+            pltpu.VMEM((n, 2, count, depth), jnp.bfloat16),
+            pltpu.VMEM((n, count, width), jnp.bfloat16),
+            pltpu.VMEM((n // 2, 2, count, width), jnp.bfloat16),
+            pltpu.VMEM((n // 2, count, width), jnp.bfloat16),
+            dma((n, 2)), dma((n, 2)), dma((n, 2)), dma((n, 2)), dma(()),
+            dma((n,)), dma((n // 2, 2)), dma((n // 2,)), dma((n // 2,)),
+        ],
+        compiler_params=pltpu.CompilerParams(
+            collective_id=1, has_side_effects=True, vmem_limit_bytes=56 * 2**20
+        ),
+        name="project",
+    )(kept, outgoing, weights, resid)
 
 
 def expand(per_head, width):
@@ -53,10 +320,9 @@
     return running, within, state
 
 
-def entering_state(running, state):
+def entering_state(running, state, logs):
     peers, position = lax.axis_size("ctx"), lax.axis_index("ctx")
     last = running[-1]
-    logs = lax.all_gather(last, "ctx")
     have, total = state, last
     reach = 1
     while reach < peers:
@@ -71,9 +337,7 @@
     return lax.ppermute(have.astype(jnp.bfloat16), "ctx", pairs)
 
 
-def mamba_mixer(x, gate, b, c, step, rate, skip, gains):
-    running, within, state = mamba_local(x, b, c, step, rate, skip)
-    entering = entering_state(running, state)
+def mamba_mixer(running, within, entering, gate, b, c, gains):
     carried = jnp.dot(c, entering, preferred_element_type=jnp.float32)
     y = within + carried * expand(jnp.exp(running), MHEAD_DIM)
     gated = y * jax.nn.silu(gate.astype(jnp.float32))
@@ -83,9 +347,8 @@
     return (scaled * gains[None, :]).astype(jnp.bfloat16)
 
 
-def attention(queries, keys, values, ctx_rank):
+def attention(queries, both, ctx_rank):
     rows = queries.shape[0]
-    both = lax.all_gather(jnp.concatenate([keys, values], axis=1), "ctx", axis=0, tiled=True)
     k, v = both[:, :HEAD_DIM], both[:, HEAD_DIM:]
     heads = queries.shape[1] // HEAD_DIM
     q = queries.reshape(rows, heads, HEAD_DIM)
@@ -122,41 +385,28 @@
 ):
     section = lax.axis_index("pipe")
     ctx_rank = lax.axis_index("ctx")
-    mamba_part = mamba_mixer(
+    peers = lax.axis_size("ctx")
+    b = take_half(ssm_in_b, 1, section)
+    c = take_half(ssm_out_c, 1, section)
+    running, within, state = mamba_local(
         take_half(ssm_input, 1, section),
-        take_half(ssm_gate, 1, section),
-        take_half(ssm_in_b, 1, section),
-        take_half(ssm_out_c, 1, section),
+        b,
+        c,
         take_half(step_size, 1, section),
         take_half(decay_rate, 0, section),
         take_half(skip_gain, 0, section),
+    )
+    kv = jnp.concatenate([take_half(keys, 1, section), take_half(values, 1, section)], axis=1)
+    both, logs = share(kv, running[-1], peers)
+    entering = entering_state(running, state, logs)
+    mamba_part = mamba_mixer(
+        running, within, entering, take_half(ssm_gate, 1, section), b, c,
         take_half(norm_gain, 0, section),
     )
-    attn_part = attention(
-        take_half(queries, 1, section),
-        take_half(keys, 1, section),
-        take_half(values, 1, section),
-        ctx_rank,
-    )
+    attn_part = attention(take_half(queries, 1, section), both, ctx_rank)
     outgoing = jnp.where(section == 0, attn_part, mamba_part)
     kept_half = jnp.where(section == 0, mamba_part, attn_part)
-    incoming = from_partner(outgoing, "pipe", 0)
-    mixed_rows = jnp.where(
-        section == 0,
-        jnp.concatenate([kept_half, incoming], axis=1),
-        jnp.concatenate([incoming, kept_half], axis=1),
-    )
-    peers = lax.axis_size("ctx")
-    rows = mixed_rows.shape[0]
-    gathered = lax.all_gather(mixed_rows, "ctx", axis=0, tiled=True)
-    partial = jnp.dot(gathered, out_weights[0], preferred_element_type=jnp.float32).astype(jnp.bfloat16)
-    pieces = lax.all_to_all(partial.reshape(peers, rows, -1), "ctx", 0, 0)
-    whole = pieces.transpose(1, 0, 2).reshape(rows, -1)
-    projected = lax.psum_scatter(whole, "tp", scatter_dimension=1, tiled=True).astype(jnp.float32)
-    own_section = (resid_in.astype(jnp.float32) + projected).astype(jnp.bfloat16)
-    received = shifted(own_section, "pipe", 1)
-    second_section = (received.astype(jnp.float32) + projected).astype(jnp.bfloat16)
-    return jnp.where(section == 0, own_section, second_section)[None]
+    return project(kept_half, outgoing, out_weights[0], resid_in, peers)[None]
 
 
 def solution(mesh):

time: 332 us -> 226 us (0.68)
  waiting for transfers between devices: 180 us -> 27.6 us
  Pallas kernels: 0 us -> 146 us
  blocking collectives: 86.6 us -> 0 us
  between operations: 13.7 us -> 0.29 us
  starting transfers between devices: 11.4 us -> 24.8 us
  matrix products: 20.3 us -> 9.78 us
    pallas_call x0 -> x2, Pallas kernels: none -> 146 us  [the longest x1 127 us: project(): pl.pallas_call(functools.partial(project_kernel, n), out_shape=jax.ShapeD...]
    all_gather x1 -> x0, waiting for transfers between devices: 124 us -> none  [per_device(): gathered = lax.all_gather(mixed_rows, 'ctx', axis=0, tiled=True)]
    all_gather x2 -> x0, blocking collectives: 56.8 us -> none  [the longest x1 33.8 us: attention(): lax.all_gather(jnp.concatenate([keys, values], axis=1), 'ctx', axis=0, ti...]
    all_to_all x1 -> x0, blocking collectives: 29.9 us -> none  [per_device(): pieces = lax.all_to_all(partial.reshape(peers, rows, -1), 'ctx', 0, 0)]
    ppermute x2 -> x0, waiting for transfers between devices: 23.3 us -> none  [the longest x1 14.7 us: shifted(): return lax.ppermute(x, axis, pairs)]
    dot_general x1 -> x0, matrix products: 9.05 us -> none  [per_device(): jnp.dot(gathered, out_weights[0], preferred_element_type=jnp.float32)]
    ppermute x3, starting transfers between devices: 6.65 us -> 15.1 us  [entering_state(): lax.ppermute(have.astype(jnp.bfloat16), 'ctx', pairs).astype(jnp.float32)]
    reduce_scatter x1 -> x0, waiting for transfers between devices: 8.35 us -> none  [per_device(): lax.psum_scatter(whole, 'tp', scatter_dimension=1, tiled=True)]
  transfers between devices with their start and end apart: 8 -> 4, of which waited for: 7 -> 3; matrix products, arithmetic and copies ran while one was open for 4% -> 5% of each run, Pallas kernels for 0% -> 8%
where the time goes in v2:
time: 226 us
  Pallas kernels  146 us (65%)
  waiting for transfers between devices  27.6 us (12%)
  starting transfers between devices  24.8 us (11%)
  matrix products  9.78 us (4%)
  local copies, waits for them, and re-layouts  8.48 us (4%)
  other arithmetic  8.45 us (4%)
    pallas_call x1, Pallas kernels, project(): pl.pallas_call(functools.partial(project_kernel, n), out_shape=jax.ShapeD...  127 us
    ppermute x3, waiting for transfers between devices, entering_state(): lax.ppermute(have.astype(jnp.bfloat16), 'ctx', pairs).astype(jnp.float32)  23.5 us
    pallas_call x1, Pallas kernels, share(): pl.pallas_call(functools.partial(share_kernel, n), out_shape=(jax.ShapeDt...  19 us
    ppermute x3, starting transfers between devices, entering_state(): lax.ppermute(have.astype(jnp.bfloat16), 'ctx', pairs).astype(jnp.float32)  15.1 us
    ppermute x1, starting transfers between devices, entering_state(): return lax.ppermute(have.astype(jnp.bfloat16), 'ctx', pairs)  9.69 us
  transfers between devices with their start and end apart: 4, of which 3 were waited for; matrix products, arithmetic and copies ran while one was open for 5% of the time, Pallas kernels for 8%

profile of v2, /device:TPU:10, one launch (start us, length us, event | category | flops | bytes accessed | tf_op | source)
XLA Modules:
  0.0 225.6 jit_solution(5139968923293274063)
XLA Ops:
  0.8 0.9 fusion.35
  3.1 1.3 constant_dynamic-slice_fusion
  4.4 1.1 fusion.47
  5.5 3.4 %collective-permute-start = (bf16[128,2048]{1,0:T(8,128)(2,1)}, bf16[128,2048]{1,0:T(8,128)(2,1)S(1)}, u32[]{:S(2)}, u32[]{:S(2)}) collective-permute-start(bf16[128,2048]{1,0:T(8,128)(2,1)} %get-tuple-element.18), channel_id=1, source_target_pairs={{0,2},{2,4},{4,6},{6,8},{8,10},{10,12},{12,14},{1,3},{3,5},{5,7},{... | collective-permute-start | bytes 1572872 | tf_op jit(solution)/shard_map/ppermute | solution.py:330
  9.5 19.0 %share.1 = (bf16[8,128,256]{2,1,0:T(8,128)(2,1)S(1)}, f32[8,8,128]{2,1,0:T(8,128)S(1)}) custom-call(bf16[128,256]{1,0:T(8,128)(2,1)S(1)} %pad_maximum_fusion.kv_ref, f32[8,128]{1,0:T(8,128)S(1)} %pad.7.log_ref), custom_call_target="tpu_custom_call" | custom-call | tf_op jit(solution)/shard_map/share/pallas_call | solution.py:58
  28.7 0.9 fusion.25
  29.6 5.1 %collective-permute-start.1 = (bf16[128,2048]{1,0:T(8,128)(2,1)}, bf16[128,2048]{1,0:T(8,128)(2,1)}, u32[]{:S(2)}, u32[]{:S(2)}) collective-permute-start(bf16[128,2048]{1,0:T(8,128)(2,1)} %fusion.25), channel_id=1, source_target_pairs={{0,4},{2,6},{4,8},{6,10},{8,12},{10,14},{1,5},{3,7},{5,9},{7,11},{... | collective-permute-start | bytes 1572872 | tf_op jit(solution)/shard_map/ppermute | solution.py:330
  35.1 1.3 fusion.2
  36.4 9.2 %collective-permute-done.1 = bf16[128,2048]{1,0:T(8,128)(2,1)} collective-permute-done((bf16[128,2048]{1,0:T(8,128)(2,1)}, bf16[128,2048]{1,0:T(8,128)(2,1)}, u32[]{:S(2)}, u32[]{:S(2)}) %collective-permute-start.1) | collective-permute-done | bytes 524320 | tf_op jit(solution)/shard_map/ppermute | solution.py:330
  45.6 1.3 fusion.28
  46.9 6.6 %collective-permute-start.2 = (bf16[128,2048]{1,0:T(8,128)(2,1)S(1)}, bf16[128,2048]{1,0:T(8,128)(2,1)S(1)}, u32[]{:S(2)}, u32[]{:S(2)}) collective-permute-start(bf16[128,2048]{1,0:T(8,128)(2,1)S(1)} %fusion.28), channel_id=1, source_target_pairs={{0,8},{2,10},{4,12},{6,14},{1,9},{3,11},{5,13},{7,15},{16,24},{18,... | collective-permute-start | bytes 1572872 | tf_op jit(solution)/shard_map/ppermute | solution.py:330
  53.5 1.7 fusion
  55.2 14.3 %collective-permute-done.2 = bf16[128,2048]{1,0:T(8,128)(2,1)S(1)} collective-permute-done((bf16[128,2048]{1,0:T(8,128)(2,1)S(1)}, bf16[128,2048]{1,0:T(8,128)(2,1)S(1)}, u32[]{:S(2)}, u32[]{:S(2)}) %collective-permute-start.2) | collective-permute-done | bytes 524320 | tf_op jit(solution)/shard_map/ppermute | solution.py:330
  69.5 2.2 add_convert_fusion
  71.7 9.7 %collective-permute-start.3 = (bf16[128,2048]{1,0:T(8,128)(2,1)}, bf16[128,2048]{1,0:T(8,128)(2,1)}, u32[]{:S(2)}, u32[]{:S(2)}) collective-permute-start(bf16[128,2048]{1,0:T(8,128)(2,1)} %add_convert_fusion), channel_id=1, source_target_pairs={{0,2},{2,4},{4,6},{6,8},{8,10},{10,12},{12,14},{1,3},{3,5},{5,7},{... | collective-permute-start | bytes 1572872 | tf_op jit(solution)/shard_map/ppermute | solution.py:337
  81.4 2.1 divide_convert_fusion
  83.5 1.0 copy.20
  85.3 2.1 fusion.11
  87.4 1.3 copy.21
  88.9 4.1 %collective-permute-done.3 = bf16[128,2048]{1,0:T(8,128)(2,1)} collective-permute-done((bf16[128,2048]{1,0:T(8,128)(2,1)}, bf16[128,2048]{1,0:T(8,128)(2,1)}, u32[]{:S(2)}, u32[]{:S(2)}) %collective-permute-start.3) | collective-permute-done | bytes 524320 | tf_op jit(solution)/shard_map/ppermute | solution.py:337
  93.1 2.2 multiply_reduce_fusion
  95.3 1.3 broadcast_select_fusion
  96.6 127.0 %project.1 = bf16[128,2048]{1,0:T(8,128)(2,1)} custom-call(bf16[128,2048]{1,0:T(8,128)(2,1)} %get-tuple-element.12.kept, bf16[128,2048]{1,0:T(8,128)(2,1)} %get-tuple-element.11.outgoing, bf16[4096,512]{1,0:T(8,128)(2,1)} %bitcast.46, bf16[128,2048]{1,0:T(8,128)(2,1)} %resid.1), custom_call_target="tpu_custom_call" | custom-call | tf_op jit(solution)/shard_map/project/pallas_call | solution.py:280
  223.7 1.9 copy.36
  (46 shorter events, 4.2 us)
Async XLA Ops:
  0.0 4.4 %copy-start = (bf16[128,256]{1,0:T(8,128)(2,1)S(1)}, bf16[128,256]{1,0:T(8,128)(2,1)}, u32[]{:S(2)}) copy-start(bf16[128,256]{1,0:T(8,128)(2,1)} %param.16) | copy-start | bytes 196612
  0.0 9.4 %copy-start.1 = (bf16[128,256]{1,0:T(8,128)(2,1)S(1)}, bf16[128,256]{1,0:T(8,128)(2,1)}, u32[]{:S(2)}) copy-start(bf16[128,256]{1,0:T(8,128)(2,1)} %param.24) | copy-start | bytes 196612
  0.0 9.4 %copy-start.2 = (bf16[128,256]{1,0:T(8,128)(2,1)S(1)}, bf16[128,256]{1,0:T(8,128)(2,1)}, u32[]{:S(2)}) copy-start(bf16[128,256]{1,0:T(8,128)(2,1)} %param.23) | copy-start | bytes 196612
  5.5 23.1 %collective-permute-start = (bf16[128,2048]{1,0:T(8,128)(2,1)}, bf16[128,2048]{1,0:T(8,128)(2,1)S(1)}, u32[]{:S(2)}, u32[]{:S(2)}) collective-permute-start(bf16[128,2048]{1,0:T(8,128)(2,1)} %get-tuple-element.18), channel_id=1, source_target_pairs={{0,2},{2,4},{4,6},{6,8},{8,10},{10,12},{12,14},{1,3},{3,5},{5,7},{... | collective-permute-start | bytes 1572872 | tf_op jit(solution)/shard_map/ppermute | solution.py:330
  29.6 16.0 %collective-permute-start.1 = (bf16[128,2048]{1,0:T(8,128)(2,1)}, bf16[128,2048]{1,0:T(8,128)(2,1)}, u32[]{:S(2)}, u32[]{:S(2)}) collective-permute-start(bf16[128,2048]{1,0:T(8,128)(2,1)} %fusion.25), channel_id=1, source_target_pairs={{0,4},{2,6},{4,8},{6,10},{8,12},{10,14},{1,5},{3,7},{5,9},{7,11},{... | collective-permute-start | bytes 1572872 | tf_op jit(solution)/shard_map/ppermute | solution.py:330
  46.9 22.6 %collective-permute-start.2 = (bf16[128,2048]{1,0:T(8,128)(2,1)S(1)}, bf16[128,2048]{1,0:T(8,128)(2,1)S(1)}, u32[]{:S(2)}, u32[]{:S(2)}) collective-permute-start(bf16[128,2048]{1,0:T(8,128)(2,1)S(1)} %fusion.28), channel_id=1, source_target_pairs={{0,8},{2,10},{4,12},{6,14},{1,9},{3,11},{5,13},{7,15},{16,24},{18,... | collective-permute-start | bytes 1572872 | tf_op jit(solution)/shard_map/ppermute | solution.py:330
  71.7 21.4 %collective-permute-start.3 = (bf16[128,2048]{1,0:T(8,128)(2,1)}, bf16[128,2048]{1,0:T(8,128)(2,1)}, u32[]{:S(2)}, u32[]{:S(2)}) collective-permute-start(bf16[128,2048]{1,0:T(8,128)(2,1)} %add_convert_fusion), channel_id=1, source_target_pairs={{0,2},{2,4},{4,6},{6,8},{8,10},{10,12},{12,14},{1,3},{3,5},{5,7},{... | collective-permute-start | bytes 1572872 | tf_op jit(solution)/shard_map/ppermute | solution.py:337
  81.4 3.8 %copy-start.3 = (bf16[128,256]{1,0:T(8,128)(2,1)S(1)}, bf16[128,256]{1,0:T(8,128)(2,1)}, u32[]{:S(2)}) copy-start(bf16[128,256]{1,0:T(8,128)(2,1)} %param.17) | copy-start | bytes 196612
  83.5 5.2 %copy-start.4 = (f32[64]{0:T(128)S(1)}, f32[64]{0:T(128)}, u32[]{:S(2)}) copy-start(f32[64]{0:T(128)} %param.20) | copy-start | bytes 772
  84.5 10.8 %dynamic-slice-start = ((f32[4096]{0:T(1024)}, s32[]{:T(128)}), f32[2048]{0:T(1024)S(1)}, s32[]{:S(2)}) async-start(f32[4096]{0:T(1024)} %param.21, s32[]{:T(128)} %select_n.45), calls=%async_computation | async-start | bytes 16896 | tf_op jit(solution)/shard_map/dynamic_slice | solution.py:368

commit v3 on v2

--- a/solution.py
+++ b/solution.py
@@ -73,18 +73,19 @@
 
 
 def project_kernel(
-    n, kept, outgoing, weights, resid, out,
-    rows, staged, parts, first,
-    row_recv, up_send, down_send, side_send, pipe_send, part_send, part_recv, first_send, first_recv,
+    n, kept, outgoing, w_own, w_side, resid, out,
+    rows, held, given, taken, staged, parts, first,
+    row_recv, up_send, down_send, pair_send, give_send, give_recv,
+    part_send, part_recv, first_send, first_recv,
 ):
     pipe, me, tp = (lax.axis_index(a) for a in ("pipe", "ctx", "tp"))
     line, half_n = n // 2, n // 2
-    pos = me // 2
-    side = me + 1 - 2 * lax.rem(me, 2)
-    owner_tp, own_chunk = me // half_n, lax.rem(me, half_n)
-    other = 1 - pipe
-    width = weights.shape[1]
-    depth = kept.shape[1]
+    pos, member = me // 2, lax.rem(me, 2)
+    side = me + 1 - 2 * member
+    other, sibling = 1 - pipe, 1 - tp
+    target = pos * 2 + tp
+    owner_tp, own_chunk = target // half_n, lax.rem(target, half_n)
+    width = w_own.shape[1]
 
     barrier = pltpu.get_barrier_semaphore()
     here = me * 2 + tp
@@ -93,98 +94,106 @@
         pl.semaphore_signal(
             barrier, inc=1, device_id=(pipe, there // 2, lax.rem(there, 2)), device_id_type=MESH
         )
-    pl.semaphore_signal(barrier, inc=1, device_id=(other, me, tp), device_id_type=MESH)
-    rows[me, pipe] = kept[...]
-    pl.semaphore_wait(barrier, 2 * n)
-
-    def hop(c, h, sem, ctx):
-        return pltpu.make_async_remote_copy(
-            rows.at[c, h], rows.at[c, h], sem.at[c, h], row_recv.at[c, h],
-            device_id=(pipe, ctx, tp), device_id_type=MESH,
-        )
-
-    def cross(h):
-        return pltpu.make_async_remote_copy(
-            outgoing, rows.at[me, h], pipe_send, row_recv.at[me, h],
-            device_id=(other, me, tp), device_id_type=MESH,
-        )
+    for ctx in (me, side):
+        pl.semaphore_signal(barrier, inc=1, device_id=(other, ctx, tp), device_id_type=MESH)
+
+    @pl.when(member == pipe)
+    def _():
+        rows[me] = kept[...]
+
+    pl.semaphore_wait(barrier, 2 * n + 1)
 
     up, down = jnp.minimum(me + 2, n - 1), jnp.maximum(me - 2, 0)
     can_up, can_down = pos + 1 < line, pos > 0
 
+    def hop(c, sem, ctx):
+        return pltpu.make_async_remote_copy(
+            rows.at[c], rows.at[c], sem.at[c], row_recv.at[c],
+            device_id=(pipe, ctx, tp), device_id_type=MESH,
+        )
+
+    def keep_copy():
+        return pltpu.make_async_remote_copy(
+            kept, rows.at[me], pair_send.at[0], row_recv.at[me],
+            device_id=(pipe, side, tp), device_id_type=MESH,
+        )
+
+    def cross(ctx):
+        return pltpu.make_async_remote_copy(
+            outgoing, rows.at[me], pair_send.at[1], row_recv.at[me],
+            device_id=(other, ctx, tp), device_id_type=MESH,
+        )
+
+    @pl.when(member == pipe)
+    def _():
+        cross(me).start()
+
+    @pl.when(member != pipe)
+    def _():
+        keep_copy().start()
+        cross(side).start()
+
+    def forward(s, start):
+        for which in range(2):
+            base = me if which == 0 else side
+            for way in range(2):
+                c = base - 2 * s if way == 0 else base + 2 * s
+                ok = (c >= 0) & (c < n)
+                if way == 1:
+                    ok = ok & (s > 0)
+
+                @pl.when(ok)
+                def _():
+                    if start:
+                        if which == 0:
+
+                            @pl.when((s > 0) | (member != pipe))
+                            def _():
+                                hop(c, up_send, up).wait_recv()
+                        else:
+                            hop(c, up_send, up).wait_recv()
+
+                    @pl.when(can_up & ((s == 0) | (way == 0)))
+                    def _():
+                        copy = hop(c, up_send, up)
+                        copy.start() if start else copy.wait_send()
+
+                    @pl.when(can_down & ((s == 0) | (way == 1)))
+                    def _():
+                        copy = hop(c, down_send, down)
+                        copy.start() if start else copy.wait_send()
+
+    def give_copy(c):
+        return pltpu.make_async_remote_copy(
+            given.at[c], taken.at[c], give_send.at[c], give_recv.at[c],
+            device_id=(pipe, me, sibling), device_id_type=MESH,
+        )
+
     def part_copy(c):
         return pltpu.make_async_remote_copy(
-            staged.at[c], parts.at[own_chunk, tp], part_send.at[c], part_recv.at[own_chunk, tp],
+            staged.at[c], parts.at[own_chunk, member],
+            part_send.at[c], part_recv.at[own_chunk, member],
             device_id=(pipe, c, owner_tp), device_id_type=MESH,
         )
 
     def is_mine(c):
         return (c == me) & (owner_tp == tp)
 
-    cross(pipe).start()
-
-    def forward(s, act):
-        @pl.when(s == 0)
-        def _():
-            for turn in range(2):
-                h = pipe if turn == 0 else other
-                if turn == 1:
-                    act(cross(other), None)
-
-                @pl.when(can_up)
-                def _():
-                    act(None, hop(me, h, up_send, up))
-
-                @pl.when(can_down)
-                def _():
-                    act(None, hop(me, h, down_send, down))
-
-                act(None, hop(me, h, side_send, side))
-
-        @pl.when((s > 0) & (s < line))
-        def _():
-            for turn in range(2):
-                h = pipe if turn == 0 else other
-                below, above = me - 2 * s, me + 2 * s
-
-                @pl.when(below >= 0)
-                def _():
-                    act(hop(below, h, up_send, up), None)
-
-                    @pl.when(can_up)
-                    def _():
-                        act(None, hop(below, h, up_send, up))
-
-                    act(None, hop(below, h, side_send, side))
-
-                @pl.when(above < n)
-                def _():
-                    act(hop(above, h, down_send, down), None)
-
-                    @pl.when(can_down)
-                    def _():
-                        act(None, hop(above, h, down_send, down))
-
-                    act(None, hop(above, h, side_send, side))
-
-    def go(arrived, leaving):
-        if arrived is not None:
-            arrived.wait_recv()
-        if leaving is not None:
-            leaving.start()
-
-    def drain(arrived, leaving):
-        if leaving is not None:
-            leaving.wait_send()
-
     def multiply(c):
-        total = jnp.dot(rows[c, 0], weights[:depth], preferred_element_type=jnp.float32)
-        total += jnp.dot(rows[c, 1], weights[depth:], preferred_element_type=jnp.float32)
-        piece = total.astype(jnp.bfloat16)
+        mine = jnp.dot(rows[c], w_own[...], preferred_element_type=jnp.float32)
+        theirs = jnp.dot(rows[c], w_side[...], preferred_element_type=jnp.float32)
+        straight = member == tp
+        held[c] = jnp.where(straight, mine, theirs)
+        given[c] = jnp.where(straight, theirs, mine).astype(jnp.bfloat16)
+        give_copy(c).start()
+
+    def pass_on(c):
+        give_copy(c).wait_recv()
+        piece = (held[c] + taken[c].astype(jnp.float32)).astype(jnp.bfloat16)
 
         @pl.when(is_mine(c))
         def _():
-            parts[own_chunk, tp] = piece
+            parts[own_chunk, member] = piece
 
         @pl.when(jnp.logical_not(is_mine(c)))
         def _():
@@ -192,30 +201,26 @@
             part_copy(c).start()
 
     def turn(s, carry):
-        forward(s, go)
-
-        def block(k, carry):
-            late = k // 2
-            dist = s - late
-            centre = me + late * (side - me)
-            c = centre + (2 * lax.rem(k, 2) - 1) * 2 * dist
-            ok = (dist >= 0) & (dist < line) & (c >= 0) & (c < n)
-            ok = ok & ((dist > 0) | (lax.rem(k, 2) == 0))
-
-            @pl.when(ok)
-            def _():
-                @pl.when(late == 1)
+        forward(s, True)
+
+        def each(act):
+            def block(k, carry):
+                base = me + (k // 2) * (side - me)
+                c = base + (2 * lax.rem(k, 2) - 1) * 2 * s
+
+                @pl.when((c >= 0) & (c < n) & ((s > 0) | (lax.rem(k, 2) == 0)))
                 def _():
-                    for h in range(2):
-                        hop(c, h, side_send, side).wait_recv()
-
-                multiply(c)
-
-            return carry
-
-        return lax.fori_loop(0, 4, block, carry)
-
-    lax.fori_loop(0, line + 1, turn, 0)
+                    act(c)
+
+                return carry
+
+            return block
+
+        lax.fori_loop(0, 4, each(multiply), 0)
+        lax.fori_loop(0, 4, each(pass_on), 0)
+        return carry
+
+    lax.fori_loop(0, line, turn, 0)
 
     def first_copy(q):
         return pltpu.make_async_remote_copy(
@@ -225,12 +230,13 @@
 
     for q in range(half_n):
         source = tp * half_n + q
-        for t in range(2):
-
-            @pl.when(jnp.logical_not((source == me) & (tp == t)))
+        for m in range(2):
+            from_ctx = source // 2 * 2 + m
+
+            @pl.when(jnp.logical_not((from_ctx == me) & (lax.rem(source, 2) == tp)))
             def _():
                 pltpu.make_async_remote_copy(
-                    parts.at[q, t], parts.at[q, t], part_send.at[0], part_recv.at[q, t],
+                    parts.at[q, m], parts.at[q, m], part_send.at[0], part_recv.at[q, m],
                     device_id=(pipe, side, tp), device_id_type=MESH,
                 ).wait_recv()
 
@@ -249,15 +255,24 @@
             first_copy(q).wait_recv()
             out[:, columns] = (first[q].astype(jnp.float32) + total).astype(jnp.bfloat16)
 
-    cross(pipe).wait_send()
+    @pl.when(member == pipe)
+    def _():
+        cross(me).wait_send()
+
+    @pl.when(member != pipe)
+    def _():
+        keep_copy().wait_send()
+        cross(side).wait_send()
 
     def finish(s, carry):
-        forward(s, drain)
+        forward(s, False)
         return carry
 
     lax.fori_loop(0, line, finish, 0)
 
     def sent(c, carry):
+        give_copy(c).wait_send()
+
         @pl.when(jnp.logical_not(is_mine(c)))
         def _():
             part_copy(c).wait_send()
@@ -272,29 +287,33 @@
             first_copy(q).wait_send()
 
 
-def project(kept, outgoing, weights, resid, n):
+def project(kept, outgoing, w_own, w_side, resid, n):
     vmem = pl.BlockSpec(memory_space=pltpu.VMEM)
     count, depth = kept.shape
-    width = weights.shape[1]
+    width = w_own.shape[1]
     dma = pltpu.SemaphoreType.DMA
+    block = (count, width)
     return pl.pallas_call(
         functools.partial(project_kernel, n),
         out_shape=jax.ShapeDtypeStruct(resid.shape, jnp.bfloat16),
-        in_specs=[vmem] * 4,
+        in_specs=[vmem] * 5,
         out_specs=vmem,
         scratch_shapes=[
-            pltpu.VMEM((n, 2, count, depth), jnp.bfloat16),
-            pltpu.VMEM((n, count, width), jnp.bfloat16),
-            pltpu.VMEM((n // 2, 2, count, width), jnp.bfloat16),
-            pltpu.VMEM((n // 2, count, width), jnp.bfloat16),
-            dma((n, 2)), dma((n, 2)), dma((n, 2)), dma((n, 2)), dma(()),
+            pltpu.VMEM((n, count, depth), jnp.bfloat16),
+            pltpu.VMEM((n, *block), jnp.float32),
+            pltpu.VMEM((n, *block), jnp.bfloat16),
+            pltpu.VMEM((n, *block), jnp.bfloat16),
+            pltpu.VMEM((n, *block), jnp.bfloat16),
+            pltpu.VMEM((n // 2, 2, *block), jnp.bfloat16),
+            pltpu.VMEM((n // 2, *block), jnp.bfloat16),
+            dma((n,)), dma((n,)), dma((n,)), dma((2,)), dma((n,)), dma((n,)),
             dma((n,)), dma((n // 2, 2)), dma((n // 2,)), dma((n // 2,)),
         ],
         compiler_params=pltpu.CompilerParams(
             collective_id=1, has_side_effects=True, vmem_limit_bytes=56 * 2**20
         ),
         name="project",
-    )(kept, outgoing, weights, resid)
+    )(kept, outgoing, w_own, w_side, resid)
 
 
 def expand(per_head, width):
@@ -322,19 +341,19 @@
 
 def entering_state(running, state, logs):
     peers, position = lax.axis_size("ctx"), lax.axis_index("ctx")
-    last = running[-1]
-    have, total = state, last
+    span = jnp.arange(peers)
+    own = jnp.exp(jnp.repeat(running[-1], MHEAD_DIM))[None, :]
+    before = jnp.zeros_like(state)
     reach = 1
     while reach < peers:
         pairs = [(i, i + reach) for i in range(peers - reach)]
-        got = lax.ppermute(have.astype(jnp.bfloat16), "ctx", pairs).astype(jnp.float32)
-        have = have + jnp.exp(jnp.repeat(total, MHEAD_DIM))[None, :] * got
-        span = jnp.arange(peers)
-        inside = (span <= position) & (span > position - 2 * reach)
-        total = jnp.sum(jnp.where(inside[:, None], logs, 0.0), axis=0)
+        sent = (state + own * before).astype(jnp.bfloat16)
+        got = lax.ppermute(sent, "ctx", pairs).astype(jnp.float32)
+        inside = (span < position) & (span > position - reach)
+        through = jnp.sum(jnp.where(inside[:, None], logs, 0.0), axis=0)
+        before = before + jnp.exp(jnp.repeat(through, MHEAD_DIM))[None, :] * got
         reach *= 2
-    pairs = [(i, i + 1) for i in range(peers - 1)]
-    return lax.ppermute(have.astype(jnp.bfloat16), "ctx", pairs)
+    return before.astype(jnp.bfloat16)
 
 
 def mamba_mixer(running, within, entering, gate, b, c, gains):
@@ -386,6 +405,11 @@
     section = lax.axis_index("pipe")
     ctx_rank = lax.axis_index("ctx")
     peers = lax.axis_size("ctx")
+    member = lax.rem(ctx_rank, 2)
+    w_own = take_half(out_weights[0], 0, member)
+    w_side = lax.ppermute(
+        take_half(out_weights[0], 0, 1 - member), "ctx", [(i, i ^ 1) for i in range(peers)]
+    )
     b = take_half(ssm_in_b, 1, section)
     c = take_half(ssm_out_c, 1, section)
     running, within, state = mamba_local(
@@ -406,7 +430,7 @@
     attn_part = attention(take_half(queries, 1, section), both, ctx_rank)
     outgoing = jnp.where(section == 0, attn_part, mamba_part)
     kept_half = jnp.where(section == 0, mamba_part, attn_part)
-    return project(kept_half, outgoing, out_weights[0], resid_in, peers)[None]
+    return project(kept_half, outgoing, w_own, w_side, resid_in, peers)[None]
 
 
 def solution(mesh):

time: 226 us -> 247 us (1.093)
  the two profiles are of different devices: /device:TPU:10 before, /device:TPU:26 now
where the time goes in v3:
time: 247 us; the launch traced here: 246 us
  Pallas kernels  178 us (72%)
  waiting for transfers between devices  29.7 us (12%)
  local copies, waits for them, and re-layouts  13.4 us (5%)
  matrix products  10.9 us (4%)
  other arithmetic  7.61 us (3%)
  starting transfers between devices  5.98 us (2%)
    pallas_call x1, Pallas kernels, project(): pl.pallas_call(functools.partial(project_kernel, n), out_shape=jax.ShapeD...  119 us
    pallas_call x1, Pallas kernels, share(): pl.pallas_call(functools.partial(share_kernel, n), out_shape=(jax.ShapeDt...  59.5 us
    ppermute x3, waiting for transfers between devices, entering_state(): got = lax.ppermute(sent, 'ctx', pairs).astype(jnp.float32)  29.7 us
    dynamic_slice x8, local copies, waits for them, and re-layouts, take_half(): return lax.dynamic_slice_in_dim(array, section * width, width, axis_dim)  7.67 us
    ppermute x3, starting transfers between devices, entering_state(): got = lax.ppermute(sent, 'ctx', pairs).astype(jnp.float32)  5.98 us
  transfers between devices with their start and end apart: 4, of which 2 were waited for; matrix products, arithmetic and copies ran while one was open for 10% of the time, Pallas kernels for 24%

profile of v3, /device:TPU:26, one launch (start us, length us, event | category | flops | bytes accessed | tf_op | source)
XLA Modules:
  0.0 246.3 jit_solution(9562479919142659184)
XLA Ops:
  0.0 0.8 dynamic_slice.47
  0.8 0.9 fusion.36
  1.9 0.8 exponential_multiply_fusion
  3.3 1.3 constant_dynamic-slice_fusion
  4.6 1.1 add_convert_fusion.3
  5.7 3.4 %collective-permute-start = (bf16[128,2048]{1,0:T(8,128)(2,1)}, bf16[128,2048]{1,0:T(8,128)(2,1)}, u32[]{:S(2)}, u32[]{:S(2)}) collective-permute-start(bf16[128,2048]{1,0:T(8,128)(2,1)} %get-tuple-element.21), channel_id=1, source_target_pairs={{0,2},{2,4},{4,6},{6,8},{8,10},{10,12},{12,14},{1,3},{3,5},{5,7},{... | collective-permute-start | bytes 1572872 | tf_op jit(solution)/shard_map/ppermute | solution.py:351
  9.2 4.5 %dynamic-slice_bitcast_fusion = (bf16[2048,512]{1,0:T(8,128)(2,1)}, bf16[2048,512]{1,0:T(8,128)(2,1)}) fusion(bf16[1,4096,512]{2,1,0:T(8,128)(2,1)} %param.25, s32[]{:T(128)S(6)} %select_n.65, s32[]{:T(128)S(6)} %select_n.64), kind=kLoop, calls=%fused_computation.10 | loop fusion | bytes 8388616 | tf_op jit(solution)/shard_map/dynamic_slice | solution.py:387
  14.1 59.5 %share.1 = (bf16[8,128,256]{2,1,0:T(8,128)(2,1)S(1)}, f32[8,8,128]{2,1,0:T(8,128)S(1)}) custom-call(bf16[128,256]{1,0:T(8,128)(2,1)S(1)} %pad_maximum_fusion.kv_ref, f32[8,128]{1,0:T(8,128)S(1)} %pad.7.log_ref), custom_call_target="tpu_custom_call" | custom-call | tf_op jit(solution)/shard_map/share/pallas_call | solution.py:58
  74.1 1.3 fusion.2
  75.4 1.2 add_convert_fusion.2
  76.6 1.3 collective-permute-start.1
  77.9 1.7 fusion
  79.6 12.7 %collective-permute-done.1 = bf16[128,2048]{1,0:T(8,128)(2,1)S(1)} collective-permute-done((bf16[128,2048]{1,0:T(8,128)(2,1)S(1)}, bf16[128,2048]{1,0:T(8,128)(2,1)S(1)}, u32[]{:S(2)}, u32[]{:S(2)}) %collective-permute-start.1) | collective-permute-done | bytes 524320 | tf_op jit(solution)/shard_map/ppermute | solution.py:351
  92.3 2.3 add_convert_fusion.1
  94.6 1.3 collective-permute-start.2
  95.9 2.1 divide_convert_fusion
  98.0 1.1 copy.20
  100.1 3.0 %fusion.11 = f32[32,64,128]{2,1,0:T(8,128)} fusion(bf16[128,32,64]{0,2,1:T(8,128)(2,1)} %bitcast.53, f32[32,128]{1,0:T(8,128)S(1)} %get-tuple-element.17, f32[32,128]{1,0:T(8,128)S(1)} %bitcast.55, f32[128,128]{1,0:T(8,128)S(1)} %fusion.32, pred[128,128]{1,0:T(8,128)(4,1)S(1)} %iota_compare_fusion.1), kind=kOutput, calls=%fused_computation.18 | convolution fusion | flops 69730304 | bytes 1687552 | tf_op jit(solution)/shard_map/hts,shp->thp/dot_general | solution.py:333
  103.1 1.6 copy.21
  104.9 17.0 %collective-permute-done.2 = bf16[128,2048]{1,0:T(8,128)(2,1)} collective-permute-done((bf16[128,2048]{1,0:T(8,128)(2,1)}, bf16[128,2048]{1,0:T(8,128)(2,1)}, u32[]{:S(2)}, u32[]{:S(2)}) %collective-permute-start.2) | collective-permute-done | bytes 524320 | tf_op jit(solution)/shard_map/ppermute | solution.py:351
  121.9 2.5 %multiply_reduce_fusion = (f32[128]{0:T(128)S(1)}, f32[128,2048]{1,0:T(8,128)S(1)}) fusion(bf16[128,4096]{1,0:T(8,128)(2,1)} %param.15, s32[]{:T(128)} %select_n.54, f32[128,2048]{1,0:T(8,128)S(1)} %copy.23, bf16[128,2048]{1,0:T(8,128)(2,1)} %collective-permute-done.2, bf16[128,2048]{1,0:T(8,128)(2,1)} %copy-done.1, ...), kind=kOutput, calls=%fused_computation.26 | convolution fusion | flops 72875904 | bytes 5833224 | tf_op jit(solution)/shard_map/dot_general | solution.py:360
  124.4 1.3 broadcast_select_fusion
  125.7 118.7 %project.1 = bf16[128,2048]{1,0:T(8,128)(2,1)} custom-call(bf16[128,2048]{1,0:T(8,128)(2,1)} %get-tuple-element.15.kept, bf16[128,2048]{1,0:T(8,128)(2,1)} %get-tuple-element.14.outgoing, bf16[2048,512]{1,0:T(8,128)(2,1)} %get-tuple-element.13.w_own, bf16[2048,512]{1,0:T(8,128)(2,1)} %collective-permute-done.3.w_side, bf16[128,2048]{1,0:T(8,128)(2,1)} %resid.1), custom_call_target="tpu_custom_call" | custom-call | tf_op jit(solution)/shard_map/project/pallas_call | solution.py:296
  244.4 1.9 copy.36
  (53 shorter events, 2.8 us)
Async XLA Ops:
  0.0 4.6 %copy-start = (bf16[128,256]{1,0:T(8,128)(2,1)S(1)}, bf16[128,256]{1,0:T(8,128)(2,1)}, u32[]{:S(2)}) copy-start(bf16[128,256]{1,0:T(8,128)(2,1)} %param.16) | copy-start | bytes 196612
  2.9 11.1 %copy-start.2 = (bf16[128,256]{1,0:T(8,128)(2,1)S(1)}, bf16[128,256]{1,0:T(8,128)(2,1)}, u32[]{:S(2)}) copy-start(bf16[128,256]{1,0:T(8,128)(2,1)} %param.24) | copy-start | bytes 196612
  2.9 11.1 %copy-start.3 = (bf16[128,256]{1,0:T(8,128)(2,1)S(1)}, bf16[128,256]{1,0:T(8,128)(2,1)}, u32[]{:S(2)}) copy-start(bf16[128,256]{1,0:T(8,128)(2,1)} %param.23) | copy-start | bytes 196612
  5.7 69.6 %collective-permute-start = (bf16[128,2048]{1,0:T(8,128)(2,1)}, bf16[128,2048]{1,0:T(8,128)(2,1)}, u32[]{:S(2)}, u32[]{:S(2)}) collective-permute-start(bf16[128,2048]{1,0:T(8,128)(2,1)} %get-tuple-element.21), channel_id=1, source_target_pairs={{0,2},{2,4},{4,6},{6,8},{8,10},{10,12},{12,14},{1,3},{3,5},{5,7},{... | collective-permute-start | bytes 1572872 | tf_op jit(solution)/shard_map/ppermute | solution.py:351
  13.6 112.0 %collective-permute-start.3 = (bf16[2048,512]{1,0:T(8,128)(2,1)}, bf16[2048,512]{1,0:T(8,128)(2,1)}, u32[]{:S(2)}, u32[]{:S(2)}) collective-permute-start(bf16[2048,512]{1,0:T(8,128)(2,1)} %get-tuple-element.12), channel_id=1, source_target_pairs={{0,2},{2,0},{4,6},{6,4},{8,10},{10,8},{12,14},{14,12},{1,3},{3,1},... | collective-permute-start | bytes 6291464 | tf_op jit(solution)/shard_map/ppermute | solution.py:410
  76.6 15.7 %collective-permute-start.1 = (bf16[128,2048]{1,0:T(8,128)(2,1)S(1)}, bf16[128,2048]{1,0:T(8,128)(2,1)S(1)}, u32[]{:S(2)}, u32[]{:S(2)}) collective-permute-start(bf16[128,2048]{1,0:T(8,128)(2,1)S(1)} %add_convert_fusion.2), channel_id=1, source_target_pairs={{0,4},{2,6},{4,8},{6,10},{8,12},{10,14},{1,5},{3,7},{5,9},{7,11},{... | collective-permute-start | bytes 1572872 | tf_op jit(solution)/shard_map/ppermute | solution.py:351
  92.3 2.3 copy-start.1
  94.6 27.2 %collective-permute-start.2 = (bf16[128,2048]{1,0:T(8,128)(2,1)}, bf16[128,2048]{1,0:T(8,128)(2,1)}, u32[]{:S(2)}, u32[]{:S(2)}) collective-permute-start(bf16[128,2048]{1,0:T(8,128)(2,1)} %add_convert_fusion.1), channel_id=1, source_target_pairs={{0,8},{2,10},{4,12},{6,14},{1,9},{3,11},{5,13},{7,15},{16,24},{18,... | collective-permute-start | bytes 1572872 | tf_op jit(solution)/shard_map/ppermute | solution.py:351
  95.9 4.0 %copy-start.4 = (bf16[128,256]{1,0:T(8,128)(2,1)S(1)}, bf16[128,256]{1,0:T(8,128)(2,1)}, u32[]{:S(2)}) copy-start(bf16[128,256]{1,0:T(8,128)(2,1)} %param.17) | copy-start | bytes 196612
  98.0 6.6 %copy-start.5 = (f32[64]{0:T(128)S(1)}, f32[64]{0:T(128)}, u32[]{:S(2)}) copy-start(f32[64]{0:T(128)} %param.20) | copy-start | bytes 772
  99.4 25.0 %dynamic-slice-start = ((f32[4096]{0:T(1024)}, s32[]{:T(128)}), f32[2048]{0:T(1024)S(1)}, s32[]{:S(2)}) async-start(f32[4096]{0:T(1024)} %param.21, s32[]{:T(128)} %select_n.54), calls=%async_computation | async-start | bytes 16896 | tf_op jit(solution)/shard_map/dynamic_slice | solution.py:387

commit v4 on v2

--- a/solution.py
+++ b/solution.py
@@ -322,19 +322,19 @@
 
 def entering_state(running, state, logs):
     peers, position = lax.axis_size("ctx"), lax.axis_index("ctx")
-    last = running[-1]
-    have, total = state, last
+    span = jnp.arange(peers)
+    own = jnp.exp(jnp.repeat(running[-1], MHEAD_DIM))[None, :]
+    before = jnp.zeros_like(state)
     reach = 1
     while reach < peers:
         pairs = [(i, i + reach) for i in range(peers - reach)]
-        got = lax.ppermute(have.astype(jnp.bfloat16), "ctx", pairs).astype(jnp.float32)
-        have = have + jnp.exp(jnp.repeat(total, MHEAD_DIM))[None, :] * got
-        span = jnp.arange(peers)
-        inside = (span <= position) & (span > position - 2 * reach)
-        total = jnp.sum(jnp.where(inside[:, None], logs, 0.0), axis=0)
+        sent = (state + own * before).astype(jnp.bfloat16)
+        got = lax.ppermute(sent, "ctx", pairs).astype(jnp.float32)
+        inside = (span < position) & (span > position - reach)
+        through = jnp.sum(jnp.where(inside[:, None], logs, 0.0), axis=0)
+        before = before + jnp.exp(jnp.repeat(through, MHEAD_DIM))[None, :] * got
         reach *= 2
-    pairs = [(i, i + 1) for i in range(peers - 1)]
-    return lax.ppermute(have.astype(jnp.bfloat16), "ctx", pairs)
+    return before.astype(jnp.bfloat16)
 
 
 def mamba_mixer(running, within, entering, gate, b, c, gains):

time: 226 us -> 209 us (0.925)
  waiting for transfers between devices: 27.6 us -> 15.6 us
  starting transfers between devices: 24.8 us -> 16 us
  Pallas kernels: 146 us -> 151 us
  other arithmetic: 8.45 us -> 5.3 us
    ppermute x4 -> x3, waiting for transfers between devices: 27.6 us -> 15.6 us  [entering_state(): got = lax.ppermute(sent, 'ctx', pairs).astype(jnp.float32)]
    ppermute x4 -> x3, starting transfers between devices: 24.8 us -> 16 us  [entering_state(): got = lax.ppermute(sent, 'ctx', pairs).astype(jnp.float32)]
    pallas_call x1, Pallas kernels: 127 us -> 132 us  [project(): pl.pallas_call(functools.partial(project_kernel, n), out_shape=jax.ShapeD...]
    convert_element_type x3 -> x2, other arithmetic: 4.4 us -> 1.23 us  [entering_state(): sent = (state + own * before).astype(jnp.bfloat16)]
  transfers between devices with their start and end apart: 4 -> 3, of which waited for: 3 -> 2; matrix products, arithmetic and copies ran while one was open for 5% -> 6% of each run, Pallas kernels for 8% -> 9%
where the time goes in v4:
time: 209 us
  Pallas kernels  151 us (72%)
  starting transfers between devices  16 us (8%)
  waiting for transfers between devices  15.6 us (7%)
  matrix products  10.4 us (5%)
  local copies, waits for them, and re-layouts  9.73 us (5%)
  other arithmetic  5.3 us (3%)
    pallas_call x1, Pallas kernels, project(): pl.pallas_call(functools.partial(project_kernel, n), out_shape=jax.ShapeD...  132 us
    pallas_call x1, Pallas kernels, share(): pl.pallas_call(functools.partial(share_kernel, n), out_shape=(jax.ShapeDt...  19.1 us
    ppermute x3, starting transfers between devices, entering_state(): got = lax.ppermute(sent, 'ctx', pairs).astype(jnp.float32)  16 us
    ppermute x3, waiting for transfers between devices, entering_state(): got = lax.ppermute(sent, 'ctx', pairs).astype(jnp.float32)  15.6 us
  transfers between devices with their start and end apart: 3, of which 2 were waited for; matrix products, arithmetic and copies ran while one was open for 6% of the time, Pallas kernels for 9%

profile of v4, /device:TPU:10, one launch (start us, length us, event | category | flops | bytes accessed | tf_op | source)
XLA Modules:
  0.0 208.7 jit_solution(10629274923950398134)
XLA Ops:
  0.0 0.8 dynamic_slice.37
  0.8 0.9 fusion.36
  1.9 0.8 exponential_multiply_fusion
  3.0 0.3 copy.22
  3.3 1.3 constant_dynamic-slice_fusion
  4.6 1.1 add_convert_fusion.3
  5.7 3.4 %collective-permute-start = (bf16[128,2048]{1,0:T(8,128)(2,1)}, bf16[128,2048]{1,0:T(8,128)(2,1)S(1)}, u32[]{:S(2)}, u32[]{:S(2)}) collective-permute-start(bf16[128,2048]{1,0:T(8,128)(2,1)} %get-tuple-element.19), channel_id=1, source_target_pairs={{0,2},{2,4},{4,6},{6,8},{8,10},{10,12},{12,14},{1,3},{3,5},{5,7},{... | collective-permute-start | bytes 1572872 | tf_op jit(solution)/shard_map/ppermute | solution.py:332
  9.6 19.1 %share.1 = (bf16[8,128,256]{2,1,0:T(8,128)(2,1)S(1)}, f32[8,8,128]{2,1,0:T(8,128)S(1)}) custom-call(bf16[128,256]{1,0:T(8,128)(2,1)S(1)} %pad_maximum_fusion.kv_ref, f32[8,128]{1,0:T(8,128)S(1)} %pad.7.log_ref), custom_call_target="tpu_custom_call" | custom-call | tf_op jit(solution)/shard_map/share/pallas_call | solution.py:58
  29.1 1.3 fusion.2
  30.6 5.2 %collective-permute-start.1 = (bf16[128,2048]{1,0:T(8,128)(2,1)S(1)}, bf16[128,2048]{1,0:T(8,128)(2,1)S(1)}, u32[]{:S(2)}, u32[]{:S(2)}) collective-permute-start(bf16[128,2048]{1,0:T(8,128)(2,1)S(1)} %add_convert_fusion.2), channel_id=1, source_target_pairs={{0,4},{2,6},{4,8},{6,10},{8,12},{10,14},{1,5},{3,7},{5,9},{7,11},{... | collective-permute-start | bytes 1572872 | tf_op jit(solution)/shard_map/ppermute | solution.py:332
  35.8 1.7 fusion
  37.5 8.8 %collective-permute-done.1 = bf16[128,2048]{1,0:T(8,128)(2,1)S(1)} collective-permute-done((bf16[128,2048]{1,0:T(8,128)(2,1)S(1)}, bf16[128,2048]{1,0:T(8,128)(2,1)S(1)}, u32[]{:S(2)}, u32[]{:S(2)}) %collective-permute-start.1) | collective-permute-done | bytes 524320 | tf_op jit(solution)/shard_map/ppermute | solution.py:332
  46.3 1.1 add_convert_fusion.1
  47.4 7.4 %collective-permute-start.2 = (bf16[128,2048]{1,0:T(8,128)(2,1)}, bf16[128,2048]{1,0:T(8,128)(2,1)}, u32[]{:S(2)}, u32[]{:S(2)}) collective-permute-start(bf16[128,2048]{1,0:T(8,128)(2,1)} %add_convert_fusion.1), channel_id=1, source_target_pairs={{0,8},{2,10},{4,12},{6,14},{1,9},{3,11},{5,13},{7,15},{16,24},{18,... | collective-permute-start | bytes 1572872 | tf_op jit(solution)/shard_map/ppermute | solution.py:332
  54.7 2.1 divide_convert_fusion
  56.8 1.0 copy.20
  58.2 1.3 copy.23
  59.8 2.1 fusion.11
  61.9 1.4 copy.21
  63.5 6.8 %collective-permute-done.2 = bf16[128,2048]{1,0:T(8,128)(2,1)} collective-permute-done((bf16[128,2048]{1,0:T(8,128)(2,1)}, bf16[128,2048]{1,0:T(8,128)(2,1)}, u32[]{:S(2)}, u32[]{:S(2)}) %collective-permute-start.2) | collective-permute-done | bytes 524320 | tf_op jit(solution)/shard_map/ppermute | solution.py:332
  70.3 2.8 %multiply_reduce_fusion = (f32[128]{0:T(128)S(1)}, f32[128,2048]{1,0:T(8,128)S(1)}) fusion(bf16[128,4096]{1,0:T(8,128)(2,1)} %param.15, s32[]{:T(128)} %select_n.48, f32[128,2048]{1,0:T(8,128)} %copy.23, bf16[128,2048]{1,0:T(8,128)(2,1)} %collective-permute-done.2, bf16[128,2048]{1,0:T(8,128)(2,1)S(1)} %collective-permute-done.1, ...), kind=kOutput, calls=%fused_computation.24 | convolution fusion | flops 72875904 | bytes 5833224 | tf_op jit(solution)/shard_map/dot_general | solution.py:341
  73.1 1.3 broadcast_select_fusion
  74.4 132.3 %project.1 = bf16[128,2048]{1,0:T(8,128)(2,1)} custom-call(bf16[128,2048]{1,0:T(8,128)(2,1)} %get-tuple-element.13.kept, bf16[128,2048]{1,0:T(8,128)(2,1)} %get-tuple-element.12.outgoing, bf16[4096,512]{1,0:T(8,128)(2,1)} %bitcast.45, bf16[128,2048]{1,0:T(8,128)(2,1)} %resid.1), custom_call_target="tpu_custom_call" | custom-call | tf_op jit(solution)/shard_map/project/pallas_call | solution.py:280
  206.8 1.9 copy.36
  (48 shorter events, 2.3 us)
Async XLA Ops:
  0.0 4.6 %copy-start = (bf16[128,256]{1,0:T(8,128)(2,1)S(1)}, bf16[128,256]{1,0:T(8,128)(2,1)}, u32[]{:S(2)}) copy-start(bf16[128,256]{1,0:T(8,128)(2,1)} %param.16) | copy-start | bytes 196612
  0.0 9.5 %copy-start.1 = (bf16[128,256]{1,0:T(8,128)(2,1)S(1)}, bf16[128,256]{1,0:T(8,128)(2,1)}, u32[]{:S(2)}) copy-start(bf16[128,256]{1,0:T(8,128)(2,1)} %param.24) | copy-start | bytes 196612
  0.0 9.5 %copy-start.2 = (bf16[128,256]{1,0:T(8,128)(2,1)S(1)}, bf16[128,256]{1,0:T(8,128)(2,1)}, u32[]{:S(2)}) copy-start(bf16[128,256]{1,0:T(8,128)(2,1)} %param.23) | copy-start | bytes 196612
  5.7 24.7 %collective-permute-start = (bf16[128,2048]{1,0:T(8,128)(2,1)}, bf16[128,2048]{1,0:T(8,128)(2,1)S(1)}, u32[]{:S(2)}, u32[]{:S(2)}) collective-permute-start(bf16[128,2048]{1,0:T(8,128)(2,1)} %get-tuple-element.19), channel_id=1, source_target_pairs={{0,2},{2,4},{4,6},{6,8},{8,10},{10,12},{12,14},{1,3},{3,5},{5,7},{... | collective-permute-start | bytes 1572872 | tf_op jit(solution)/shard_map/ppermute | solution.py:332
  30.6 15.7 %collective-permute-start.1 = (bf16[128,2048]{1,0:T(8,128)(2,1)S(1)}, bf16[128,2048]{1,0:T(8,128)(2,1)S(1)}, u32[]{:S(2)}, u32[]{:S(2)}) collective-permute-start(bf16[128,2048]{1,0:T(8,128)(2,1)S(1)} %add_convert_fusion.2), channel_id=1, source_target_pairs={{0,4},{2,6},{4,8},{6,10},{8,12},{10,14},{1,5},{3,7},{5,9},{7,11},{... | collective-permute-start | bytes 1572872 | tf_op jit(solution)/shard_map/ppermute | solution.py:332
  47.4 22.9 %collective-permute-start.2 = (bf16[128,2048]{1,0:T(8,128)(2,1)}, bf16[128,2048]{1,0:T(8,128)(2,1)}, u32[]{:S(2)}, u32[]{:S(2)}) collective-permute-start(bf16[128,2048]{1,0:T(8,128)(2,1)} %add_convert_fusion.1), channel_id=1, source_target_pairs={{0,8},{2,10},{4,12},{6,14},{1,9},{3,11},{5,13},{7,15},{16,24},{18,... | collective-permute-start | bytes 1572872 | tf_op jit(solution)/shard_map/ppermute | solution.py:332
  54.7 4.9 %copy-start.3 = (bf16[128,256]{1,0:T(8,128)(2,1)S(1)}, bf16[128,256]{1,0:T(8,128)(2,1)}, u32[]{:S(2)}) copy-start(bf16[128,256]{1,0:T(8,128)(2,1)} %param.17) | copy-start | bytes 196612
  56.8 6.5 %copy-start.4 = (f32[64]{0:T(128)S(1)}, f32[64]{0:T(128)}, u32[]{:S(2)}) copy-start(f32[64]{0:T(128)} %param.20) | copy-start | bytes 772
  58.1 15.0 %dynamic-slice-start = ((f32[4096]{0:T(1024)}, s32[]{:T(128)}), f32[2048]{0:T(1024)S(1)}, s32[]{:S(2)}) async-start(f32[4096]{0:T(1024)} %param.21, s32[]{:T(128)} %select_n.48), calls=%async_computation | async-start | bytes 16896 | tf_op jit(solution)/shard_map/dynamic_slice | solution.py:368

commit v5 on v4

--- a/solution.py
+++ b/solution.py
@@ -42,13 +42,25 @@
         )
 
     for k in range(1, n):
-        for copy in copies(k, me):
-            copy.start()
+
+        @pl.when(me + k < n)
+        def _():
+            for copy in copies(k, me):
+                copy.start()
+            kv_all[lax.rem(me + k, n)] = jnp.zeros_like(kv_ref)
+            log_all[lax.rem(me + k, n)] = jnp.zeros_like(log_ref)
+
     for k in range(1, n):
-        for copy in copies(k, lax.rem(me + k, n)):
-            copy.wait_recv()
-        for copy in copies(k, me):
-            copy.wait_send()
+
+        @pl.when(me + k >= n)
+        def _():
+            for copy in copies(k, lax.rem(me + k, n)):
+                copy.wait_recv()
+
+        @pl.when(me + k < n)
+        def _():
+            for copy in copies(k, me):
+                copy.wait_send()
 
 
 def share(kv, last, n):

time: 209 us -> 208 us (level)
  Pallas kernels: 151 us -> 143 us
  starting transfers between devices: 16 us -> 22 us
    ppermute x3, starting transfers between devices: 16 us -> 22 us  [entering_state(): got = lax.ppermute(sent, 'ctx', pairs).astype(jnp.float32)]
    pallas_call x1, Pallas kernels: 132 us -> 127 us  [project(): pl.pallas_call(functools.partial(project_kernel, n), out_shape=jax.ShapeD...]
    pallas_call x1, Pallas kernels: 19.1 us -> 15.7 us  [share(): pl.pallas_call(functools.partial(share_kernel, n), out_shape=(jax.ShapeDt...]
  transfers between devices with their start and end apart: 3 -> 3, of which waited for: 2 -> 2; matrix products, arithmetic and copies ran while one was open for 6% -> 6% of each run, Pallas kernels for 9% -> 8%
where the time goes in v5:
time: 208 us; the launch traced here: 207 us
  Pallas kernels  143 us (69%)
  starting transfers between devices  22 us (11%)
  waiting for transfers between devices  16.3 us (8%)
  matrix products  10.4 us (5%)
  local copies, waits for them, and re-layouts  9.73 us (5%)
  other arithmetic  5.3 us (3%)
    pallas_call x1, Pallas kernels, project(): pl.pallas_call(functools.partial(project_kernel, n), out_shape=jax.ShapeD...  127 us
    ppermute x3, starting transfers between devices, entering_state(): got = lax.ppermute(sent, 'ctx', pairs).astype(jnp.float32)  22 us
    ppermute x3, waiting for transfers between devices, entering_state(): got = lax.ppermute(sent, 'ctx', pairs).astype(jnp.float32)  16.3 us
    pallas_call x1, Pallas kernels, share(): pl.pallas_call(functools.partial(share_kernel, n), out_shape=(jax.ShapeDt...  15.7 us
  transfers between devices with their start and end apart: 3, of which 2 were waited for; matrix products, arithmetic and copies ran while one was open for 6% of the time, Pallas kernels for 8%

profile of v5, /device:TPU:10, one launch (start us, length us, event | category | flops | bytes accessed | tf_op | source)
XLA Modules:
  0.0 207.1 jit_solution(5172415935577716996)
XLA Ops:
  0.0 0.8 dynamic_slice.37
  0.8 0.9 fusion.36
  1.9 0.8 exponential_multiply_fusion
  3.0 0.3 copy.22
  3.3 1.3 constant_dynamic-slice_fusion
  4.6 1.1 add_convert_fusion.3
  5.7 3.4 %collective-permute-start = (bf16[128,2048]{1,0:T(8,128)(2,1)}, bf16[128,2048]{1,0:T(8,128)(2,1)S(1)}, u32[]{:S(2)}, u32[]{:S(2)}) collective-permute-start(bf16[128,2048]{1,0:T(8,128)(2,1)} %get-tuple-element.19), channel_id=1, source_target_pairs={{0,2},{2,4},{4,6},{6,8},{8,10},{10,12},{12,14},{1,3},{3,5},{5,7},{... | collective-permute-start | bytes 1572872 | tf_op jit(solution)/shard_map/ppermute | solution.py:344
  9.6 15.7 %share.1 = (bf16[8,128,256]{2,1,0:T(8,128)(2,1)S(1)}, f32[8,8,128]{2,1,0:T(8,128)S(1)}) custom-call(bf16[128,256]{1,0:T(8,128)(2,1)S(1)} %pad_maximum_fusion.kv_ref, f32[8,128]{1,0:T(8,128)S(1)} %pad.7.log_ref), custom_call_target="tpu_custom_call" | custom-call | tf_op jit(solution)/shard_map/share/pallas_call | solution.py:70
  25.8 1.3 fusion.2
  27.2 6.5 %collective-permute-start.1 = (bf16[128,2048]{1,0:T(8,128)(2,1)S(1)}, bf16[128,2048]{1,0:T(8,128)(2,1)S(1)}, u32[]{:S(2)}, u32[]{:S(2)}) collective-permute-start(bf16[128,2048]{1,0:T(8,128)(2,1)S(1)} %add_convert_fusion.2), channel_id=1, source_target_pairs={{0,4},{2,6},{4,8},{6,10},{8,12},{10,14},{1,5},{3,7},{5,9},{7,11},{... | collective-permute-start | bytes 1572872 | tf_op jit(solution)/shard_map/ppermute | solution.py:344
  33.7 1.7 fusion
  35.4 7.0 %collective-permute-done.1 = bf16[128,2048]{1,0:T(8,128)(2,1)S(1)} collective-permute-done((bf16[128,2048]{1,0:T(8,128)(2,1)S(1)}, bf16[128,2048]{1,0:T(8,128)(2,1)S(1)}, u32[]{:S(2)}, u32[]{:S(2)}) %collective-permute-start.1) | collective-permute-done | bytes 524320 | tf_op jit(solution)/shard_map/ppermute | solution.py:344
  42.4 1.1 add_convert_fusion.1
  43.5 12.2 %collective-permute-start.2 = (bf16[128,2048]{1,0:T(8,128)(2,1)}, bf16[128,2048]{1,0:T(8,128)(2,1)}, u32[]{:S(2)}, u32[]{:S(2)}) collective-permute-start(bf16[128,2048]{1,0:T(8,128)(2,1)} %add_convert_fusion.1), channel_id=1, source_target_pairs={{0,8},{2,10},{4,12},{6,14},{1,9},{3,11},{5,13},{7,15},{16,24},{18,... | collective-permute-start | bytes 1572872 | tf_op jit(solution)/shard_map/ppermute | solution.py:344
  55.6 2.1 divide_convert_fusion
  57.7 1.0 copy.20
  59.1 1.3 copy.23
  60.7 2.1 fusion.11
  62.8 1.4 copy.21
  64.4 9.3 %collective-permute-done.2 = bf16[128,2048]{1,0:T(8,128)(2,1)} collective-permute-done((bf16[128,2048]{1,0:T(8,128)(2,1)}, bf16[128,2048]{1,0:T(8,128)(2,1)}, u32[]{:S(2)}, u32[]{:S(2)}) %collective-permute-start.2) | collective-permute-done | bytes 524320 | tf_op jit(solution)/shard_map/ppermute | solution.py:344
  73.7 2.8 %multiply_reduce_fusion = (f32[128]{0:T(128)S(1)}, f32[128,2048]{1,0:T(8,128)S(1)}) fusion(bf16[128,4096]{1,0:T(8,128)(2,1)} %param.15, s32[]{:T(128)} %select_n.48, f32[128,2048]{1,0:T(8,128)} %copy.23, bf16[128,2048]{1,0:T(8,128)(2,1)} %collective-permute-done.2, bf16[128,2048]{1,0:T(8,128)(2,1)S(1)} %collective-permute-done.1, ...), kind=kOutput, calls=%fused_computation.24 | convolution fusion | flops 72875904 | bytes 5833224 | tf_op jit(solution)/shard_map/dot_general | solution.py:353
  76.5 1.3 broadcast_select_fusion
  77.8 127.4 %project.1 = bf16[128,2048]{1,0:T(8,128)(2,1)} custom-call(bf16[128,2048]{1,0:T(8,128)(2,1)} %get-tuple-element.13.kept, bf16[128,2048]{1,0:T(8,128)(2,1)} %get-tuple-element.12.outgoing, bf16[4096,512]{1,0:T(8,128)(2,1)} %bitcast.45, bf16[128,2048]{1,0:T(8,128)(2,1)} %resid.1), custom_call_target="tpu_custom_call" | custom-call | tf_op jit(solution)/shard_map/project/pallas_call | solution.py:292
  205.2 1.9 copy.36
  (48 shorter events, 2.3 us)
Async XLA Ops:
  0.0 4.6 %copy-start = (bf16[128,256]{1,0:T(8,128)(2,1)S(1)}, bf16[128,256]{1,0:T(8,128)(2,1)}, u32[]{:S(2)}) copy-start(bf16[128,256]{1,0:T(8,128)(2,1)} %param.16) | copy-start | bytes 196612
  0.0 9.5 %copy-start.1 = (bf16[128,256]{1,0:T(8,128)(2,1)S(1)}, bf16[128,256]{1,0:T(8,128)(2,1)}, u32[]{:S(2)}) copy-start(bf16[128,256]{1,0:T(8,128)(2,1)} %param.24) | copy-start | bytes 196612
  0.0 9.5 %copy-start.2 = (bf16[128,256]{1,0:T(8,128)(2,1)S(1)}, bf16[128,256]{1,0:T(8,128)(2,1)}, u32[]{:S(2)}) copy-start(bf16[128,256]{1,0:T(8,128)(2,1)} %param.23) | copy-start | bytes 196612
  5.7 21.3 %collective-permute-start = (bf16[128,2048]{1,0:T(8,128)(2,1)}, bf16[128,2048]{1,0:T(8,128)(2,1)S(1)}, u32[]{:S(2)}, u32[]{:S(2)}) collective-permute-start(bf16[128,2048]{1,0:T(8,128)(2,1)} %get-tuple-element.19), channel_id=1, source_target_pairs={{0,2},{2,4},{4,6},{6,8},{8,10},{10,12},{12,14},{1,3},{3,5},{5,7},{... | collective-permute-start | bytes 1572872 | tf_op jit(solution)/shard_map/ppermute | solution.py:344
  27.2 15.2 %collective-permute-start.1 = (bf16[128,2048]{1,0:T(8,128)(2,1)S(1)}, bf16[128,2048]{1,0:T(8,128)(2,1)S(1)}, u32[]{:S(2)}, u32[]{:S(2)}) collective-permute-start(bf16[128,2048]{1,0:T(8,128)(2,1)S(1)} %add_convert_fusion.2), channel_id=1, source_target_pairs={{0,4},{2,6},{4,8},{6,10},{8,12},{10,14},{1,5},{3,7},{5,9},{7,11},{... | collective-permute-start | bytes 1572872 | tf_op jit(solution)/shard_map/ppermute | solution.py:344
  43.5 30.2 %collective-permute-start.2 = (bf16[128,2048]{1,0:T(8,128)(2,1)}, bf16[128,2048]{1,0:T(8,128)(2,1)}, u32[]{:S(2)}, u32[]{:S(2)}) collective-permute-start(bf16[128,2048]{1,0:T(8,128)(2,1)} %add_convert_fusion.1), channel_id=1, source_target_pairs={{0,8},{2,10},{4,12},{6,14},{1,9},{3,11},{5,13},{7,15},{16,24},{18,... | collective-permute-start | bytes 1572872 | tf_op jit(solution)/shard_map/ppermute | solution.py:344
  55.6 4.9 %copy-start.3 = (bf16[128,256]{1,0:T(8,128)(2,1)S(1)}, bf16[128,256]{1,0:T(8,128)(2,1)}, u32[]{:S(2)}) copy-start(bf16[128,256]{1,0:T(8,128)(2,1)} %param.17) | copy-start | bytes 196612
  57.7 6.5 %copy-start.4 = (f32[64]{0:T(128)S(1)}, f32[64]{0:T(128)}, u32[]{:S(2)}) copy-start(f32[64]{0:T(128)} %param.20) | copy-start | bytes 772
  59.1 17.5 %dynamic-slice-start = ((f32[4096]{0:T(1024)}, s32[]{:T(128)}), f32[2048]{0:T(1024)S(1)}, s32[]{:S(2)}) async-start(f32[4096]{0:T(1024)} %param.21, s32[]{:T(128)} %select_n.48), calls=%async_computation | async-start | bytes 16896 | tf_op jit(solution)/shard_map/dynamic_slice | solution.py:380
